TPU v7x, 32 devices: a whole 2x2x4 slice. The times are simulated.
32 devices in a mesh: phase: 2 (over x), dp: 16 (over z, y, core).
Axes of the slice: x: 2, y: 2, z: 4, core: 2. Of those that a mesh axis runs over, the one named last changes fastest.
Arguments:
- hidden_in: bfloat16 [16384, 768], P('dp'), may hold values from -6 to 6
- out_grad: bfloat16 [16384, 768], P('dp'), may hold values from -6 to 6
- qkv_weight: bfloat16 [2, 768, 2304], P('phase'), may hold values from -0.3125 to 0.3125
- out_weight: bfloat16 [2, 768, 768], P('phase'), may hold values from -0.625 to 0.625
- rel_table: float32 [2, 256, 12], P('phase'), may hold values from -4 to 4
- norm1_gain: float32 [2, 768], P('phase'), may hold values from 0.25 to 1.75
- norm1_bias: float32 [2, 768], P('phase'), may hold values from -1.5 to 1.5
- up_weight: bfloat16 [2, 768, 3072], P('phase'), may hold values from -0.21875 to 0.21875
- down_weight: bfloat16 [2, 3072, 768], P('phase'), may hold values from -0.15625 to 0.15625
- norm2_gain: float32 [2, 768], P('phase'), may hold values from 0.25 to 1.75
- norm2_bias: float32 [2, 768], P('phase'), may hold values from -1.5 to 1.5
- seg_ids: int32 [16384], P('dp'), may hold values from 0 to 3, as said below
- pad_mask: int32 [16384], P('dp'), may hold values from 0 to 1, as said below
- rel_buckets: int32 [1023], replicated, may hold values from 0 to 255
Outputs:
- layer_out: bfloat16 [2, 16384, 768], P('phase', 'dp')
- input_grad: bfloat16 [2, 16384, 768], P('phase', 'dp')
- qkv_grad: float32 [2, 768, 2304], P('phase', 'dp')
- out_proj_grad: float32 [2, 768, 768], P('phase', 'dp')
- table_grad: float32 [2, 256, 12], P('phase', 'dp')
- norm1_gain_grad: float32 [2, 768], P('phase', 'dp')
- norm1_bias_grad: float32 [2, 768], P('phase', 'dp')
- up_grad: float32 [2, 768, 3072], P('phase', 'dp')
- down_grad: float32 [2, 3072, 768], P('phase', 'dp')
- norm2_gain_grad: float32 [2, 768], P('phase', 'dp')
- norm2_bias_grad: float32 [2, 768], P('phase', 'dp')
Inputs may be any that keep to these rules, and one draw needn't show every extreme that they name: `seg_ids`: in each aligned block of 512 slots, either every slot has number 0 (one sequence; exactly a quarter of the blocks) or slot i of the block has number i // 128. `pad_mask`: the used slots of a sequence are its first ones: at least 256 of a whole-block sequence, at least 32 of a short one.
All inputs are finite; a program needn't handle non-finite values.
Results may differ from a plain program's by a relative error of at most 0.04.
Values may be sent and summed in bfloat16 or wider, within the bound.
No kernel may reach another device: no remote copies, remote signals or barrier semaphores. Data moves between devices by JAX's collectives and lax.ppermute only.
A program may use at most 512 MiB of HBM per device.

v0:
```python
import functools

import jax
import jax.numpy as jnp
from jax import lax
from jax.experimental import pallas as pl
from jax.experimental.pallas import tpu as pltpu
from jax.sharding import PartitionSpec as P

BLOCK = 512
MICRO = 2
TILE = 128
LANES = 128
CHUNK = 512
SPAN = 2 * BLOCK
VMEM_BYTES = 58 * 1024 * 1024
SMALL_VMEM_BYTES = 20 * 1024 * 1024
NORM_LANE = 16

norm_eps = 1e-05
mask_fill = -1000000000.0
score_scale = 0.125
inv_root_two = 0.7071067811865476
inv_root_tau = 0.3989422804014327
log2_e = 1.4426950408889634
highest = lax.Precision.HIGHEST

F32 = jnp.float32
BF16 = jnp.bfloat16
ANY = pl.BlockSpec(memory_space=pl.ANY)
VMEM = pl.BlockSpec(memory_space=pltpu.VMEM)
QUICK = pl.CostEstimate(flops=1, bytes_accessed=1, transcendentals=0)
SMEM = pl.BlockSpec(memory_space=pltpu.SMEM)


def dot_nn(a, b):
    return lax.dot_general(a, b, (((1,), (0,)), ((), ())), preferred_element_type=F32)


def dot_nt(a, b):
    return lax.dot_general(a, b, (((1,), (1,)), ((), ())), preferred_element_type=F32)


def dot_tn(a, b):
    return lax.dot_general(a, b, (((0,), (0,)), ((), ())), preferred_element_type=F32)


def row_mean(rows):
    return jnp.sum(rows, -1, keepdims=True) * (1.0 / rows.shape[-1])


def normal_parts(residual):
    centred = residual - row_mean(residual)
    inv_scale = lax.rsqrt(row_mean(centred * centred) + norm_eps)
    return centred * inv_scale, inv_scale


def norm_backward(grad_rows, normal_form, inv_scale):
    first = row_mean(grad_rows)
    second = row_mean(grad_rows * normal_form)
    return inv_scale * (grad_rows - first - normal_form * second)


def gelu_parts(hidden):
    share = 0.5 + 0.5 * lax.erf(hidden * inv_root_two)
    bell = jnp.exp2(hidden * hidden * (-0.5 * log2_e))
    return hidden * share, share + hidden * bell * inv_root_tau


def half_mask(which, shape):
    lane = lax.broadcasted_iota(jnp.int32, shape, 1)
    return (lane < LANES // 2) if which == 0 else (lane >= LANES // 2)


class Copies:
    def __init__(self, sems):
        self.sems = sems
        self.used = 0
        self.stores = []

    def take(self, count=1):
        self.used += count
        return self.used - count

    def load(self, source, target):
        copy = pltpu.make_async_copy(source, target, self.sems.at[self.take()])
        copy.start()
        return copy

    def store(self, source, target, when=True):
        if when:
            self.stores.append(self.load(source, target))

    def finish(self):
        for copy in self.stores:
            copy.wait()


KEPT = (
    "xin", "qkv", "weights", "ctx", "form1", "scale1", "low1", "slope", "act", "form2", "scale2", "out",
    "bias", "outer_low", "hidden_low", "residual_low", "sums1", "sums2", "residual", "projected", "offsets", "input_grad",
)
INS = (
    "phase", "segments", "hidden_in", "received", "out_grad", "table", "padding", "buckets",
    "gain1", "shift1", "gain2", "shift2",
    "wqkv", "wout", "wup", "wdown",
)


class Layer:
    def __init__(self, refs):
        self.__dict__.update(refs)
        self.copies = Copies(self.sems)
        self.width = self.hidden_in.shape[1]
        self.inner = self.wup.shape[2]
        self.pairs = self.width // LANES
        self.stages = self.inner // (2 * CHUNK)
        self.pair_sems = self.copies.take(self.pairs)
        self.chunk_sems = [self.copies.take(self.stages) for _ in range(3)]

    def lanes_of(self, pair, part):
        return pl.ds(pl.multiple_of(part * self.width + pair * LANES, LANES), LANES)

    def stage(self, i):
        return pl.ds(pl.multiple_of(i * 2 * CHUNK, 2 * CHUNK), 2 * CHUNK)

    def build_bias(self):
        span = self.buckets.shape[1]
        bucket_ids = lax.broadcasted_iota(jnp.int32, (self.table.shape[1], span), 0)
        hot = (bucket_ids == self.buckets[...]).astype(F32)
        values = lax.dot_general(
            self.table[0], hot, (((0,), (0,)), ((), ())), precision=highest, preferred_element_type=F32
        )
        self.values_v[:, :span] = values
        self.values_v[:, span:] = jnp.zeros((values.shape[0], SPAN - span), F32)

        def one_head(head, carry):
            wide = jnp.broadcast_to(self.values_v[pl.ds(head, 1), :], (TILE, SPAN))
            self.bias_v[head] = pltpu.roll(wide, 1, 1, stride=1, stride_axis=0)
            return carry

        lax.fori_loop(0, values.shape[0], one_head, 0)
        self.copies.store(self.bias_v, self.bias)


    def rows(self, block):
        return pl.ds(block * BLOCK, BLOCK)

    def forward(self, block, keep, built):
        copies = self.copies
        rows = self.rows(block)
        load_x = copies.load(self.hidden_in.at[rows] if keep else self.received, self.x_v)
        width = self.width
        loads = [
            copies.load(self.wqkv.at[0, :, pl.ds(c, width)], self.wqkv_v.at[:, pl.ds(c, width)])
            for c in range(0, 3 * width, width)
        ]
        if not built:
            self.build_bias()
        load_x.wait()

        def load_bias(pair):
            heads = pl.ds(2 * pair, 2)
            return pltpu.make_async_copy(self.bias.at[heads], self.bias_v.at[heads], self.sems.at[self.pair_sems + pair])

        for i, c in enumerate(range(0, 3 * width, width)):
            loads[i].wait()
            if i == 2 and built:
                for pair in range(self.pairs):
                    load_bias(pair).start()
            self.qkv_v[:, c : c + width] = dot_nn(self.x_v[...], self.wqkv_v[:, c : c + width]).astype(BF16)
        copies.store(self.x_v, self.xin.at[rows])
        copies.store(self.qkv_v, self.qkv.at[rows], keep)
        weights_sem = self.sems.at[copies.take()]
        later_loads = [
            pltpu.make_async_copy(source.at[0], target, self.sems.at[copies.take()])
            for source, target in ((self.wout, self.wout_v), (self.wup, self.wup_v), (self.wdown, self.wdown_v))
        ]

        def own(pair, part, which):
            both = self.qkv_v[:, self.lanes_of(pair, part)]
            return jnp.where(half_mask(which, both.shape), both, jnp.zeros_like(both))

        single = self.segments[block * BLOCK + TILE] == self.segments[block * BLOCK]
        padding = self.padding[:, block * BLOCK : (block + 1) * BLOCK]
        tile_of = lax.broadcasted_iota(jnp.int32, (1, BLOCK), 1) // TILE
        shut = [
            jnp.where((padding == 1) & (single | (tile_of == tile)), 0.0, mask_fill) for tile in range(BLOCK // TILE)
        ]
        row_id = lax.broadcasted_iota(jnp.int32, (TILE, TILE), 0)
        diagonal = row_id == lax.broadcasted_iota(jnp.int32, (TILE, TILE), 1)

        def bias_rows(head, tile):
            at = BLOCK - tile * TILE
            rows = self.bias_v[head, :, at : at + BLOCK]
            masked = rows + shut[tile]
            own = slice(tile * TILE, (tile + 1) * TILE)
            parts = [masked[:, : own.start], jnp.where(diagonal, rows[:, own], masked[:, own]), masked[:, own.stop :]]
            return jnp.concatenate([part for part in parts if part.shape[1]], 1)

        def weigh(pair, which):
            head = 2 * pair + which
            k_own = own(pair, 1, which)
            for r in range(0, BLOCK, 2 * TILE):
                q_rows = self.qkv_v[r : r + 2 * TILE, self.lanes_of(pair, 0)] * jnp.asarray(score_scale, BF16)
                tiles = [bias_rows(head, tile) for tile in range(r // TILE, r // TILE + 2)]
                logits = dot_nt(q_rows, k_own) + jnp.concatenate(tiles, 0)
                raised = jnp.exp(logits - jnp.max(logits, -1, keepdims=True))
                share = pl.reciprocal(jnp.sum(raised, -1, keepdims=True), approx=True)
                self.weights_v[head, r : r + 2 * TILE, :] = (raised * share).astype(BF16)

        def head_pair(pair, carry):
            if built:
                load_bias(pair).wait()

            @pl.when(pair == 0)
            def _():
                for load in later_loads:
                    load.start()

            weigh(pair, 0)
            context = dot_nn(self.weights_v[2 * pair], own(pair, 2, 0))
            weigh(pair, 1)
            context += dot_nn(self.weights_v[2 * pair + 1], own(pair, 2, 1))
            self.ctx_v[:, self.lanes_of(pair, 0)] = context.astype(BF16)
            if keep:
                heads = pl.ds(2 * pair, 2)
                pltpu.make_async_copy(self.weights_v.at[heads], self.weights.at[block, heads], weights_sem).start()
            return carry

        lax.fori_loop(0, self.pairs, head_pair, 0)
        if keep:
            copies.stores.append(pltpu.make_async_copy(self.weights_v, self.weights.at[block], weights_sem))
        copies.store(self.ctx_v, self.ctx.at[rows])
        load_out, load_up, load_down = later_loads
        load_out.wait()
        self.acc_v[...] = dot_nn(self.ctx_v[...], self.wout_v[...])
        for r in range(0, BLOCK, 64):
            tile = slice(r, r + 64)
            form, scale = normal_parts(self.acc_v[tile, :] + self.x_v[tile, :].astype(F32))
            normed = form * self.gain1[...] + self.shift1[...]
            self.form1_v[tile, :] = form
            self.scale1_v[tile, :] = scale
            self.acc_v[tile, :] = normed
            self.low1_v[tile, :] = normed.astype(BF16)
        copies.store(self.form1_v, self.form1.at[rows], keep)
        copies.store(self.scale1_v, self.scale1.at[rows], keep)
        copies.store(self.low1_v, self.low1.at[rows])
        load_up.wait()
        load_down.wait()
        act_sem = self.sems.at[copies.take()]
        slope_sem = self.sems.at[copies.take()]

        def two_chunks(i, carry):
            span = self.stage(i)
            active, grade = gelu_parts(dot_nn(self.low1_v[...], self.wup_v[:, span]))
            active = active.astype(BF16)
            self.act_v[:, span] = active
            self.slope_v[:, span] = grade.astype(BF16)
            self.acc_v[...] += dot_nn(active, self.wdown_v[span, :])
            pltpu.make_async_copy(self.act_v.at[:, span], self.act.at[rows, span], act_sem).start()
            if keep:
                pltpu.make_async_copy(self.slope_v.at[:, span], self.slope.at[rows, span], slope_sem).start()
            return carry

        lax.fori_loop(0, self.stages, two_chunks, 0)
        copies.stores.append(pltpu.make_async_copy(self.act_v, self.act.at[rows], act_sem))
        if keep:
            copies.stores.append(pltpu.make_async_copy(self.slope_v, self.slope.at[rows], slope_sem))
        for r in range(0, BLOCK, 64):
            tile = slice(r, r + 64)
            form, scale = normal_parts(self.acc_v[tile, :])
            self.form2_v[tile, :] = form
            self.scale2_v[tile, :] = scale
            self.out_v[tile, :] = (form * self.gain2[...] + self.shift2[...]).astype(BF16)
        copies.store(self.out_v, self.send, keep)
        copies.store(self.out_v, self.out.at[rows])
        copies.store(self.form2_v, self.form2.at[rows], keep)
        copies.store(self.scale2_v, self.scale2.at[rows], keep)


    def chunk_loads(self, i, rows):
        span = self.stage(i)
        return [
            pltpu.make_async_copy(source, target, self.sems.at[self.chunk_sems[k] + i])
            for k, (source, target) in enumerate(
                (
                    (self.wdown.at[0, span], self.wdown_v.at[span]),
                    (self.slope.at[rows, span], self.slope_v.at[:, span]),
                    (self.wup.at[0, :, span], self.wup_v.at[:, span]),
                )
            )
        ]

    def norm_sums(self, source, form_ref, sums_ref):
        gain_sum = jnp.zeros((1, self.width), F32)
        shift_sum = jnp.zeros((1, self.width), F32)
        for r in range(0, BLOCK, 64):
            grad_rows, form = source[r : r + 64, :].astype(F32), form_ref[r : r + 64, :]
            gain_sum += jnp.sum(grad_rows * form, 0, keepdims=True)
            shift_sum += jnp.sum(grad_rows, 0, keepdims=True)
        sums_ref[...] = jnp.zeros(sums_ref.shape, F32)
        sums_ref[0:1, :] = gain_sum
        sums_ref[1:2, :] = shift_sum

    def norm_back(self, block):
        for r in range(0, BLOCK, 64):
            tile = slice(r, r + 64)
            grad_rows = self.g_v[tile, :].astype(F32) * self.gain2[...]
            grad_outer = norm_backward(grad_rows, self.form2_v[tile, :], self.scale2_v[tile, :])
            self.acc_v[tile, :] = grad_outer
            self.outer_v[tile, :] = grad_outer.astype(BF16)
        self.copies.store(self.outer_v, self.outer_low.at[self.rows(block)])

    def norm_sums_2(self, block):
        self.norm_sums(self.g_v, self.form2_v, self.sums2_v)
        self.copies.store(self.sums2_v, self.sums2.at[block])

    def ffn_back(self, block, staged=False, middle_loads=()):
        copies = self.copies
        rows = self.rows(block)
        hidden_sem = self.sems.at[copies.take()]

        def two_chunks(i, carry):
            span = self.stage(i)
            if staged:
                load_down, load_slope, load_up = self.chunk_loads(i, rows)
                load_down.wait()
                load_slope.wait()
            grad_active = dot_nt(self.outer_v[...], self.wdown_v[span, :])
            hidden = (grad_active * self.slope_v[:, span].astype(F32)).astype(BF16)
            self.slope_v[:, span] = hidden
            if staged:
                load_up.wait()

                @pl.when(i + 2 < self.stages)
                def _():
                    for load in self.chunk_loads(i + 2, rows):
                        load.start()

            self.acc_v[...] += dot_nt(hidden, self.wup_v[:, span])
            pltpu.make_async_copy(self.slope_v.at[:, span], self.hidden_low.at[rows, span], hidden_sem).start()
            return carry

        lax.fori_loop(0, self.stages, two_chunks, 0)
        copies.stores.append(pltpu.make_async_copy(self.slope_v, self.hidden_low.at[rows], hidden_sem))
        for load in middle_loads:
            load.wait()
        self.norm_sums(self.acc_v, self.form1_v, self.sums1_v)
        for r in range(0, BLOCK, 64):
            tile = slice(r, r + 64)
            grad_residual = norm_backward(
                self.acc_v[tile, :] * self.gain1[...], self.form1_v[tile, :], self.scale1_v[tile, :]
            )
            self.acc_v[tile, :] = grad_residual
            self.residual_low_v[tile, :] = grad_residual.astype(BF16)
        copies.store(self.residual_low_v, self.residual_low.at[rows])
        copies.store(self.sums1_v, self.sums1.at[block])

    def attn_back(self, block, load_pair=None, load_in=()):
        copies = self.copies
        rows = self.rows(block)
        self.dctx_v[...] = dot_nt(self.residual_low_v[...], self.wout_v[...]).astype(BF16)
        self.fold_v[:, :, 0:TILE] = jnp.zeros((2, TILE, TILE), F32)

        def head_pair(pair, carry):
            def lanes_of(part):
                return self.lanes_of(pair, part)

            q_pair, k_pair, v_pair = (self.qkv_v[:, lanes_of(part)] for part in range(3))
            grad_pair = self.dctx_v[:, lanes_of(0)]
            crossed = grad_pair.astype(F32) * self.ctx_v[:, lanes_of(0)].astype(F32)
            if load_pair is not None:
                load_pair(pair).wait()
            masks = [half_mask(which, k_pair.shape) for which in range(2)]

            def own(both, which):
                return jnp.where(masks[which], both, jnp.zeros_like(both))

            for which in range(2):
                self.square_v[which] = dot_nt(grad_pair, own(v_pair, which))
            q_grad = k_grad = v_grad = 0.0
            for which in range(2):
                head = 2 * pair + which
                delta = jnp.sum(own(crossed, which), -1, keepdims=True)
                for r in range(0, BLOCK, 64):
                    tile = slice(r, r + 64)
                    score_grad = (
                        self.weights_v[head, tile, :].astype(F32) * (self.square_v[which, tile, :] - delta[tile, :])
                    ).astype(BF16)
                    self.half_v[which, tile, :] = score_grad
                    at = BLOCK - r // TILE * TILE
                    wide = score_grad.astype(F32)
                    half = slice(r % TILE, r % TILE + 64)
                    if r < TILE:
                        self.fold_v[which, half, at : at + BLOCK] = wide
                    else:
                        self.fold_v[which, half, at : at + TILE] = wide[:, :TILE]
                        self.fold_v[which, half, at + TILE : at + BLOCK] += wide[:, TILE:]
                v_grad += dot_tn(self.weights_v[head], own(grad_pair, which))
                q_grad += dot_nn(self.half_v[which], own(k_pair, which))
                k_grad += dot_tn(self.half_v[which], own(q_pair, which))
                folded = self.fold_v[which]
                size = TILE // 2
                while size >= 8:
                    folded = folded[:size, :] + pltpu.roll(folded[size:, :], SPAN - size, 1)
                    size //= 2
                self.eighth_v[head] = folded
            self.qkv_v[:, lanes_of(0)] = (q_grad * score_scale).astype(BF16)
            self.qkv_v[:, lanes_of(1)] = (k_grad * score_scale).astype(BF16)
            self.qkv_v[:, lanes_of(2)] = v_grad.astype(BF16)
            return carry

        lax.fori_loop(0, self.pairs, head_pair, 0)
        copies.store(self.eighth_v, self.offsets.at[block])
        copies.store(self.qkv_v, self.projected.at[rows])
        for load in load_in:
            load.wait()
        self.grad_v[...] = (self.acc_v[...] + dot_nt(self.qkv_v[...], self.wqkv_v[...])).astype(BF16)
        copies.store(self.grad_v, self.send)
        copies.store(self.grad_v, self.input_grad.at[rows])


    def do_forward(self, block):
        self.forward(block, True, block > 0)

    def do_bias(self, block):
        self.build_bias()

    def do_both(self, block):
        load = self.copies.load(self.out_grad.at[self.rows(block)], self.g_v)
        self.forward(block, False, True)
        load.wait()
        self.norm_back(block)
        self.ffn_back(block)
        self.norm_sums_2(block)
        self.attn_back(block)

    def do_back(self, block):
        rows = self.rows(block)
        loads = [
            self.copies.load(source, target)
            for source, target in (
                (self.received, self.g_v),
                (self.form2.at[rows], self.form2_v),
                (self.scale2.at[rows], self.scale2_v),
                (self.slope.at[rows], self.slope_v),
                (self.wdown.at[0], self.wdown_v),
                (self.wup.at[0], self.wup_v),
                (self.form1.at[rows], self.form1_v),
                (self.scale1.at[rows], self.scale1_v),
                (self.qkv.at[rows], self.qkv_v),
                (self.weights.at[block], self.weights_v),
                (self.ctx.at[rows], self.ctx_v),
                (self.wout.at[0], self.wout_v),
                (self.wqkv.at[0], self.wqkv_v),
            )
        ]
        for load in loads:
            load.wait()
        self.norm_back(block)
        self.ffn_back(block)
        self.norm_sums_2(block)
        self.attn_back(block)

    def do_norm_back(self, block):
        rows = self.rows(block)
        loads = [
            self.copies.load(source, target)
            for source, target in (
                (self.received, self.g_v),
                (self.form2.at[rows], self.form2_v),
                (self.scale2.at[rows], self.scale2_v),
            )
        ]
        for load in loads:
            load.wait()
        self.norm_back(block)
        self.copies.store(self.acc_v, self.residual)
        self.norm_sums_2(block)

    def do_ffn_back(self, block):
        rows = self.rows(block)
        loads = [
            self.copies.load(self.outer_low.at[rows], self.outer_v),
            self.copies.load(self.residual, self.acc_v),
        ]
        for i in range(min(2, self.stages)):
            for load in self.chunk_loads(i, rows):
                load.start()
        for load in loads:
            load.wait()
        middle = [
            self.copies.load(self.form1.at[rows], self.form1_v),
            self.copies.load(self.scale1.at[rows], self.scale1_v),
        ]
        self.ffn_back(block, True, middle)
        self.copies.store(self.acc_v, self.residual)

    def do_attn_back(self, block):
        rows = self.rows(block)
        loads = [
            self.copies.load(source, target)
            for source, target in (
                (self.residual_low.at[rows], self.residual_low_v),
                (self.wout.at[0], self.wout_v),
                (self.qkv.at[rows], self.qkv_v),
                (self.ctx.at[rows], self.ctx_v),
            )
        ]

        def load_pair(pair):
            heads = pl.ds(2 * pair, 2)
            return pltpu.make_async_copy(
                self.weights.at[block, heads], self.weights_v.at[heads], self.sems.at[self.pair_sems + pair]
            )

        for pair in range(self.pairs):
            load_pair(pair).start()
        for load in loads:
            load.wait()
        last = [
            self.copies.load(self.wqkv.at[0], self.wqkv_v),
            self.copies.load(self.residual, self.acc_v),
        ]
        self.attn_back(block, load_pair, last)


def layer_kernel(work, phase_on, block, ins, outs, scratch, after_count, kept_count, *refs):
    refs_in, refs = refs[: len(ins)], refs[len(ins) + after_count + kept_count :]
    named = dict(zip(ins, refs_in)) | dict(zip(outs, refs)) | dict(zip(scratch, refs[len(outs) :]))

    @pl.when(named["phase"][0] == phase_on)
    def _():
        layer = Layer(named)
        getattr(layer, f"do_{work}")(block)
        layer.copies.finish()


def layer_step(work, phase_on, block, values, afters, kept, kept_shapes, scratch):
    specs = [SMEM] * 2 + [ANY] * 3 + [VMEM] * 7 + [ANY] * 4
    names = list(scratch)
    kept = list(kept) if kept is not None else []
    sent = jax.ShapeDtypeStruct((BLOCK, values[2].shape[1]), BF16)
    if work == "norm_back":
        names = [f"{name}_v" for name in ("g", "form2", "scale2", "acc", "outer", "sums2")]
    elif work == "bias":
        names = ["values_v", "bias_v"]
    count = len(values) + len(afters)
    results = pl.pallas_call(
        functools.partial(
            layer_kernel, work, phase_on, block, INS, KEPT + ("send",), names + ["sems"], len(afters), len(kept)
        ),
        out_shape=list(kept_shapes) + [sent],
        in_specs=specs + [ANY] * (len(afters) + len(kept)),
        out_specs=[ANY] * (len(kept_shapes) + 1),
        scratch_shapes=[pltpu.VMEM(*scratch[name]) for name in names] + [pltpu.SemaphoreType.DMA((80,))],
        input_output_aliases={count + i: i for i in range(len(kept))},
        compiler_params=pltpu.CompilerParams(vmem_limit_bytes=VMEM_BYTES),
        name=f"{work}_{phase_on}_{block}",
    )(*values, *afters, *kept)
    return dict(zip(KEPT, results)), results[-1]


def pack_kernel(ways, buckets_ref, offsets_ref, sums1_ref, sums2_ref, *refs):
    out_ref, turn_v = refs[-2:]
    row_of = lax.broadcasted_iota(jnp.int32, (8, SPAN), 0)
    lines = []
    for head in range(offsets_ref.shape[1]):
        eighth = offsets_ref[0, head] + offsets_ref[1, head]
        for size in (4, 2, 1):
            eighth = jnp.where((row_of & size) != 0, pltpu.roll(eighth, SPAN - size, 1), eighth)
        lines.append(jnp.sum(eighth, 0, keepdims=True))
    lines += [jnp.zeros((1, SPAN), F32)] * (NORM_LANE - len(lines))
    sums = pltpu.roll(jnp.concatenate(lines, 0), SPAN - 1, 1)
    span = buckets_ref.shape[1]
    buckets, depth = out_ref.shape[0] // 3, out_ref.shape[0] // ways
    share = buckets // ways
    bucket_ids = lax.broadcasted_iota(jnp.int32, (buckets, span), 0)
    hot = (bucket_ids == buckets_ref[...]).astype(F32)
    table = lax.dot_general(
        hot, sums[:, :span], (((1,), (1,)), ((), ())), precision=highest, preferred_element_type=F32
    ).astype(BF16)
    turn_v[...] = jnp.zeros(turn_v.shape, F32)
    for i, ref in enumerate((sums1_ref, sums2_ref)):
        at = NORM_LANE + 2 * i
        turn_v[at : at + 2, :] = ref[0, 0:2, :] + ref[1, 0:2, :]
    out_ref[...] = turn_v[...].T.astype(BF16)
    for i in range(ways):
        out_ref[i * depth : i * depth + share, 0:NORM_LANE] = table[i * share : (i + 1) * share, :]


def packed(ways, buckets, offset_buckets, kept, afters):
    width = kept["sums1"].shape[2]
    depth, share = width // ways, buckets // ways
    arrays = (offset_buckets, kept["offsets"], kept["sums1"], kept["sums2"])
    if depth % 16 == 0 and share % 16 == 0 and 3 * buckets == width:
        rows = pl.pallas_call(
            functools.partial(pack_kernel, ways),
            out_shape=jax.ShapeDtypeStruct((width, LANES), BF16),
            in_specs=[VMEM] * len(arrays) + [ANY] * len(afters),
            out_specs=VMEM,
            scratch_shapes=[pltpu.VMEM((LANES, width), F32)],
            compiler_params=pltpu.CompilerParams(vmem_limit_bytes=SMALL_VMEM_BYTES),
            name="pack",
        )(*arrays, *afters)
        return rows.reshape(ways, depth, LANES)
    eighths = jnp.sum(kept["offsets"], 0)
    lines = sum(jnp.roll(eighths[:, i, :], -i, 1) for i in range(8))[:, 1:]
    hot = (offset_buckets[0][None, :] == jnp.arange(buckets, dtype=jnp.int32)[:, None]).astype(F32)
    table = jnp.dot(hot, lines.T, precision=highest).reshape(ways, share, -1)
    table = jnp.pad(table, ((0, 0), (0, depth - share), (0, NORM_LANE - table.shape[2])))
    norms = jnp.concatenate([jnp.sum(kept[name], 0)[:2] for name in ("sums1", "sums2")], 0)
    norms = norms.T.reshape(ways, depth, 4)
    rows = jnp.concatenate([table, norms], 2)
    return jnp.pad(rows, ((0, 0), (0, 0), (0, LANES - rows.shape[2]))).astype(BF16)


def halve_kernel(bits, counts, after_count, through_count, me_ref, *refs):
    used = sum(counts) + len(counts)
    outs = refs[used + after_count + through_count :]
    for i, count in enumerate(counts):
        kept_refs, arrived_ref = refs[:count], refs[count]
        refs = refs[count + 1 :]
        send_ref, rest_ref = outs[2 * i : 2 * i + 2]
        mine = (me_ref[0] >> bits[i]) & 1

        def total(which):
            kept = [
                (ref[0, which, 0, 0] if len(ref.shape) == 6 else ref[0, which, 0]).astype(F32)
                for ref in kept_refs
            ]
            return jnp.concatenate(kept, 1) + arrived_ref[0, which, 0].astype(F32)

        send_ref[0, 0] = total(1 - mine).astype(send_ref.dtype)
        rest_ref[0, 0] = total(mine)


def join_kernel(kept_near, arrived_near, kept_far, arrived_far, out_ref, qkv_ref, table_ref, *refs):
    norm_refs, turn_v = refs[:-1], refs[-1]
    near = kept_near[...] + arrived_near[...].astype(F32)
    wide = out_ref.shape[1]
    share = qkv_ref.shape[1] - kept_far.shape[1]
    out_ref[...] = near[:, :wide]
    qkv_ref[:, :share] = near[:, wide : wide + share]
    qkv_ref[:, share:] = kept_far[...] + arrived_far[...].astype(F32)
    small = near[:, wide + share :]
    table_ref[...] = small[: table_ref.shape[0], : table_ref.shape[1]]
    turn_v[...] = jnp.zeros(turn_v.shape, F32)
    turn_v[: small.shape[0], :] = small
    turned = turn_v[...].T
    for i, ref in enumerate(norm_refs):
        ref[...] = turned[NORM_LANE + i : NORM_LANE + i + 1, : ref.shape[1]]


class Share:
    def __init__(self, parts, order):
        self.parts = parts
        self.order = order[1:]
        self.left = sorted(order)
        self.depth = parts[0].shape[1]
        self.wide = sum(part.shape[2] for part in parts)
        self.mine = None
        self.swap(order[0], self.of_core(1 - (lax.axis_index("dp") & 1)))

    def of_core(self, core):
        halves = [
            lax.dynamic_index_in_dim(
                part.reshape((part.shape[0] // 2, 2) + part.shape[1:]), core, 1, keepdims=False
            )
            for part in self.parts
        ]
        return halves[0] if len(halves) == 1 else jnp.concatenate(halves, 2)

    def swap(self, bit, theirs):
        count = lax.axis_size("dp")
        self.left.remove(bit)
        self.sent = theirs
        self.arrived = lax.ppermute(theirs, "dp", [(i, i ^ (1 << bit)) for i in range(count)])

    def total(self):
        kept = self.of_core(lax.axis_index("dp") & 1) if self.mine is None else self.mine
        return kept.astype(F32) + self.arrived.astype(F32)

    def split_at(self):
        bit = self.order[0]
        axis = len(self.left) - 1 - self.left.index(bit)
        return bit, 2**axis, 2 ** (len(self.left) - 1 - axis)

    def halve(self):
        bit, above, below = self.split_at()
        self.order = self.order[1:]
        split = self.total().reshape(above, 2, below, self.depth, self.wide)
        here = (lax.axis_index("dp") >> bit) & 1
        theirs = lax.dynamic_index_in_dim(split, 1 - here, 1, keepdims=False).astype(BF16)
        mine = lax.dynamic_index_in_dim(split, here, 1, keepdims=False)
        self.mine = mine.reshape(-1, self.depth, self.wide)
        self.swap(bit, theirs.reshape(-1, self.depth, self.wide))


def halve_all(me, shares, afters=(), through=()):
    if any(share.depth % 16 for share in shares):
        for share in shares:
            share.halve()
        return through
    ins, in_specs, outs, out_specs, bits, counts = [], [], [], [], [], []
    for share in shares:
        bit, above, below = share.split_at()
        bits.append(bit)

        def halves(wide, b=below):
            return pl.BlockSpec((1, 2, 1, share.depth, wide), lambda i, me: (i // b, 0, i % b, 0, 0))

        if share.mine is None:
            counts.append(len(share.parts))
            for part in share.parts:
                wide = part.shape[2]
                ins.append(part.reshape(above, 2, below, 2, share.depth, wide))
                in_specs.append(
                    pl.BlockSpec(
                        (1, 2, 1, 1, share.depth, wide),
                        lambda i, me, b=below: (i // b, 0, i % b, me[0] & 1, 0, 0),
                    )
                )
        else:
            counts.append(1)
            ins.append(share.mine.reshape(above, 2, below, share.depth, share.wide))
            in_specs.append(halves(share.wide))
        ins.append(share.arrived.reshape(above, 2, below, share.depth, share.wide))
        in_specs.append(halves(share.wide))
        outs += [
            jax.ShapeDtypeStruct((above, below, share.depth, share.wide), kind) for kind in (BF16, F32)
        ]
        out_specs += [
            pl.BlockSpec((1, 1, share.depth, share.wide), lambda i, me, b=below: (i // b, i % b, 0, 0))
        ] * 2
        steps = above * below
    results = pl.pallas_call(
        functools.partial(halve_kernel, tuple(bits), tuple(counts), len(afters), len(through)),
        grid_spec=pltpu.PrefetchScalarGridSpec(
            num_scalar_prefetch=1,
            grid=(steps,),
            in_specs=in_specs + [ANY] * (len(afters) + len(through)),
            out_specs=out_specs + [ANY] * len(through),
        ),
        out_shape=outs + [jax.ShapeDtypeStruct(array.shape, array.dtype) for array in through],
        input_output_aliases={
            1 + len(ins) + len(afters) + i: len(outs) + i for i in range(len(through))
        },
        compiler_params=pltpu.CompilerParams(vmem_limit_bytes=VMEM_BYTES if through else SMALL_VMEM_BYTES),
        name="halve",
    )(me, *ins, *afters, *through)
    for i, share in enumerate(shares):
        share.order = share.order[1:]
        share.mine = results[2 * i + 1].reshape(-1, share.depth, share.wide)
        share.swap(bits[i], results[2 * i].reshape(-1, share.depth, share.wide))
    return results[len(outs) :]


def joined(near, far, width, table_shape):
    parts = [x[0] for share in (near, far) for x in (share.mine, share.arrived)]
    shapes = [(near.depth, width), (near.depth, near.wide + far.wide - width - LANES), table_shape]
    shapes += [(1, near.depth)] * 4
    return pl.pallas_call(
        join_kernel,
        out_shape=[jax.ShapeDtypeStruct(dims, F32) for dims in shapes],
        in_specs=[VMEM] * len(parts),
        out_specs=[VMEM] * len(shapes),
        scratch_shapes=[pltpu.VMEM((LANES, LANES), F32)],
        compiler_params=pltpu.CompilerParams(vmem_limit_bytes=SMALL_VMEM_BYTES),
        name="join",
    )(*parts)


def passed_along(x, axis, by):
    length = lax.axis_size(axis)
    pairs = [(i, i + by) for i in range(length) if 0 <= i + by < length]
    return lax.ppermute(x, axis, pairs)


def shards(
    hidden_in, out_grad, qkv_weight, out_weight, rel_table, norm1_gain, norm1_bias,
    up_weight, down_weight, norm2_gain, norm2_bias, seg_ids, pad_mask, rel_buckets,
):
    phase = lax.axis_index("phase").astype(jnp.int32).reshape(1)
    ways = lax.axis_size("dp")
    slots, width = hidden_in.shape
    inner = up_weight.shape[2]
    buckets, heads = rel_table.shape[1:]

    def shape(dims, kind):
        return jax.ShapeDtypeStruct(dims, kind)

    rows_of = {
        "xin": (width, BF16), "qkv": (3 * width, BF16), "ctx": (width, BF16), "form1": (width, F32),
        "scale1": (1, F32), "low1": (width, BF16), "slope": (inner, BF16), "act": (inner, BF16),
        "form2": (width, F32), "scale2": (1, F32), "out": (width, BF16),
        "outer_low": (width, BF16), "hidden_low": (inner, BF16), "residual_low": (width, BF16),
        "projected": (3 * width, BF16), "input_grad": (width, BF16),
    }
    kept_shapes = [
        shape((slots, rows_of[name][0]), rows_of[name][1])
        if name in rows_of
        else {
            "weights": shape((MICRO, heads, BLOCK, BLOCK), BF16),
            "sums1": shape((MICRO, 8, width), F32),
            "sums2": shape((MICRO, 8, width), F32),
            "residual": shape((BLOCK, width), F32),
            "offsets": shape((MICRO, heads, 8, SPAN), F32),
            "bias": shape((heads, TILE, SPAN), F32),
        }[name]
        for name in KEPT
    ]
    in_forward = ("qkv", "ctx", "form1", "scale1", "low1", "slope", "act", "form2", "scale2", "out")
    scratch = {f"{name}_v": ((BLOCK, rows_of[name][0]), rows_of[name][1]) for name in in_forward}
    scratch |= {
        name: ((BLOCK, width), BF16) for name in ("x_v", "g_v", "outer_v", "residual_low_v", "dctx_v", "grad_v")
    }
    scratch |= {
        "weights_v": ((heads, BLOCK, BLOCK), BF16), "acc_v": ((BLOCK, width), F32), "square_v": ((2, BLOCK, BLOCK), F32),
        "values_v": ((heads, SPAN), F32), "bias_v": ((heads, TILE, SPAN), F32), "sums1_v": ((8, width), F32), "sums2_v": ((8, width), F32),
        "wqkv_v": ((width, 3 * width), BF16), "wout_v": ((width, width), BF16), "wup_v": ((width, inner), BF16),
        "wdown_v": ((inner, width), BF16), "fold_v": ((2, TILE, SPAN), F32), "eighth_v": ((heads, 8, SPAN), F32),
        "half_v": ((2, BLOCK, BLOCK), BF16),
    }

    def step(work, phase_on, block, received, kept, afters=()):
        values = (
            phase, seg_ids, hidden_in, received, out_grad, rel_table, pad_mask[None, :], rel_buckets[None, :],
            norm1_gain, norm1_bias, norm2_gain, norm2_bias, qkv_weight, out_weight, up_weight, down_weight,
        )
        in_place = None if kept is None else [kept[name] for name in KEPT]
        return layer_step(work, phase_on, block, values, list(afters), in_place, kept_shapes, scratch)

    kept, sent = step("forward", 0, 0, hidden_in, None)
    first = passed_along(sent, "phase", 1)
    kept, _ = step("bias", 1, 0, hidden_in, kept)
    kept, sent = step("forward", 0, 1, hidden_in, kept)
    second = passed_along(sent, "phase", 1)
    kept, sent = step("both", 1, 0, first, kept)
    first_back = passed_along(sent, "phase", -1)
    kept, sent = step("both", 1, 1, second, kept)
    second_back = passed_along(sent, "phase", -1)
    kept, _ = step("back", 0, 0, first_back, kept)
    kept, _ = step("norm_back", 0, 1, second_back, kept)

    bits = ways.bit_length() - 1
    near_first = list(range(bits))
    far_first = [0] + list(range(2, bits)) + [1] if bits > 1 else near_first
    me = lax.axis_index("dp").astype(jnp.int32).reshape(1)

    def weight_grad(left, right):
        product = dot_tn(left, right).astype(BF16)
        return product.reshape(ways, product.shape[0] // ways, product.shape[1])

    down = Share([weight_grad(kept["act"], kept["outer_low"])], far_first)
    kept, _ = step("ffn_back", 0, 1, hidden_in, kept, [down.sent])
    (hidden_low,) = halve_all(me, [down], through=[kept["hidden_low"]])
    up = Share([weight_grad(kept["low1"], hidden_low)], near_first)
    out_part = weight_grad(kept["ctx"], kept["residual_low"])
    kept["hidden_low"] = hidden_low
    halve_all(me, [up])
    kept, _ = step("attn_back", 0, 1, hidden_in, kept, [down.sent, up.sent])
    (projected,) = halve_all(me, [down], through=[kept["projected"]])
    far = Share([weight_grad(kept["xin"], projected[:, width:])], far_first)
    (slots_in,) = halve_all(me, [up], [down.sent, far.sent], [kept["xin"]])
    near_part = weight_grad(slots_in, projected[:, :width])
    small = packed(ways, buckets, rel_buckets[None, :], kept, [far.sent])
    near = Share([out_part, near_part, small], near_first)
    halve_all(me, [down])
    halve_all(me, [near, far], [up.sent])
    halve_all(me, [up])
    halve_all(me, [near, far], [up.sent])
    while down.order:
        halve_all(me, [down, up])
    while near.order:
        halve_all(me, [near, far])
    down_share = down.total()[0]
    up_share = up.total()[0]
    out_share, qkv_share, table_share, *norm_shares = joined(near, far, width, (buckets // ways, heads))
    return (
        kept["out"][None],
        kept["input_grad"][None],
        qkv_share[None],
        out_share[None],
        table_share[None],
        norm_shares[0],
        norm_shares[1],
        up_share[None],
        down_share[None],
        norm_shares[2],
        norm_shares[3],
    )


def solution(mesh):
    return jax.shard_map(
        shards,
        mesh=mesh,
        in_specs=(
            P("dp", None),
            P("dp", None),
            P("phase", None, None),
            P("phase", None, None),
            P("phase", None, None),
            P("phase", None),
            P("phase", None),
            P("phase", None, None),
            P("phase", None, None),
            P("phase", None),
            P("phase", None),
            P("dp"),
            P("dp"),
            P(),
        ),
        out_specs=(
            P("phase", "dp", None),
            P("phase", "dp", None),
            P("phase", "dp", None),
            P("phase", "dp", None),
            P("phase", "dp", None),
            P("phase", "dp"),
            P("phase", "dp"),
            P("phase", "dp", None),
            P("phase", "dp", None),
            P("phase", "dp"),
            P("phase", "dp"),
        ),
        check_vma=False,
    )
```

profile of v0, /device:TPU:0, one launch (start us, length us, event | category | flops | bytes accessed | tf_op | source)
XLA Modules:
  0.0 341.1 jit_solution(5316803842974644159)
XLA Ops:
  2.1 24.4 %forward_0_0.1 = (bf16[1024,768]{1,0:T(8,128)(2,1)}, bf16[1024,2304]{1,0:T(8,128)(2,1)}, bf16[2,12,512,512]{3,2,1,0:T(8,128)(2,1)}, bf16[1024,768]{1,0:T(8,128)(...) custom-call(s32[1]{0:T(128)} %bitcast.refs_0_, ...), custom_call_target="tpu_custom_call" | custom-call | tf_op jit(solution)/shard_map/forward_0_0/pallas_call | solution.py:550
  27.9 1.8 bias_1_0.1
  29.7 23.6 %forward_0_1.1 = (bf16[1024,768]{1,0:T(8,128)(2,1)}, bf16[1024,2304]{1,0:T(8,128)(2,1)}, bf16[2,12,512,512]{3,2,1,0:T(8,128)(2,1)}, bf16[1024,768]{1,0:T(8,128)(...) custom-call(s32[1]{0:T(128)} %bitcast.refs_0_, ...), custom_call_target="tpu_custom_call", output_to_operand_aliasing={{0}: (16, {}), {1}: (17, {}), {2}: (18, {}), {3}: (19, {}),... | custom-call | tf_op jit(solution)/shard_map/forward_0_1/pallas_call | solution.py:550
  55.6 11.3 %both_1_0.1 = (bf16[1024,768]{1,0:T(8,128)(2,1)}, bf16[1024,2304]{1,0:T(8,128)(2,1)}, bf16[2,12,512,512]{3,2,1,0:T(8,128)(2,1)}, bf16[1024,768]{1,0:T(8,128)(2,1...) custom-call(s32[1]{0:T(128)} %bitcast.refs_0_, ...), custom_call_target="tpu_custom_call", output_to_operand_aliasing={{0}: (16, {}), {1}: (17, {}), {2}: (18, {}), {3}: (19, {}),... | custom-call | tf_op jit(solution)/shard_map/both_1_0/pallas_call | solution.py:550
  68.2 4.4 %collective-permute-done.refs_3_ = bf16[512,768]{1,0:T(8,128)(2,1)S(1)} collective-permute-done((bf16[512,768]{1,0:T(8,128)(2,1)}, bf16[512,768]{1,0:T(8,128)(2,1)S(1)}, u32[]{:S(2)}, u32[]{:S(2)}) %collective-permute-start) | collective-permute-done | bytes 786464 | tf_op jit(solution)/shard_map/ppermute | solution.py:778
  73.5 1.9 both_1_1.1
  76.7 42.8 %collective-permute-done.3.refs_3_ = bf16[512,768]{1,0:T(8,128)(2,1)S(1)} collective-permute-done((bf16[512,768]{1,0:T(8,128)(2,1)}, bf16[512,768]{1,0:T(8,128)(2,1)S(1)}, u32[]{:S(2)}, u32[]{:S(2)}) %collective-permute-start.3) | collective-permute-done | bytes 786464 | tf_op jit(solution)/shard_map/ppermute | solution.py:778
  120.4 32.0 %back_0_0.1 = (bf16[1024,768]{1,0:T(8,128)(2,1)}, bf16[1024,2304]{1,0:T(8,128)(2,1)}, bf16[2,12,512,512]{3,2,1,0:T(8,128)(2,1)}, bf16[1024,768]{1,0:T(8,128)(2,1...) custom-call(s32[1]{0:T(128)} %bitcast.refs_0_, ...), custom_call_target="tpu_custom_call", output_to_operand_aliasing={{0}: (16, {}), {1}: (17, {}), {2}: (18, {}), {3}: (19, {}),... | custom-call | tf_op jit(solution)/shard_map/back_0_0/pallas_call | solution.py:550
  152.4 11.6 %collective-permute-done.2.refs_3_ = bf16[512,768]{1,0:T(8,128)(2,1)S(1)} collective-permute-done((bf16[512,768]{1,0:T(8,128)(2,1)}, bf16[512,768]{1,0:T(8,128)(2,1)S(1)}, u32[]{:S(2)}, u32[]{:S(2)}) %collective-permute-start.2) | collective-permute-done | bytes 786464 | tf_op jit(solution)/shard_map/ppermute | solution.py:778
  164.9 5.4 %norm_back_0_1.1 = (bf16[1024,768]{1,0:T(8,128)(2,1)}, bf16[1024,2304]{1,0:T(8,128)(2,1)}, bf16[2,12,512,512]{3,2,1,0:T(8,128)(2,1)}, bf16[1024,768]{1,0:T(8,128...) custom-call(s32[1]{0:T(128)} %bitcast.refs_0_, ...), custom_call_target="tpu_custom_call", output_to_operand_aliasing={{0}: (16, {}), {1}: (17, {}), {2}: (18, {}), {3}: (19, {}),... | custom-call | tf_op jit(solution)/shard_map/norm_back_0_1/pallas_call | solution.py:550
  170.3 7.8 %convolution_convert_fusion.1 = bf16[3072,768]{1,0:T(8,128)(2,1)S(1)} fusion(bf16[1024,3072]{1,0:T(8,128)(2,1)} %get-tuple-element.368.refs_25_, bf16[1024,768]{1,0:T(8,128)(2,1)} %get-tuple-element.369.refs_30_), kind=kOutput, calls=%fused_computation.1 | convolution fusion | flops 4834197504 | bytes 12582912 | tf_op jit(solution)/shard_map/dot_general | solution.py:45
  178.1 1.8 dynamic-slice_bitcast_fusion.1.refs_16_
  181.0 14.5 %ffn_back_0_1.1 = (bf16[1024,768]{1,0:T(8,128)(2,1)}, bf16[1024,2304]{1,0:T(8,128)(2,1)}, bf16[2,12,512,512]{3,2,1,0:T(8,128)(2,1)}, bf16[1024,768]{1,0:T(8,128)...) custom-call(s32[1]{0:T(128)} %bitcast.refs_0_, ...), custom_call_target="tpu_custom_call", output_to_operand_aliasing={{0}: (17, {}), {1}: (18, {}), {2}: (19, {}), {3}: (20, {}),... | custom-call | tf_op jit(solution)/shard_map/ffn_back_0_1/pallas_call | solution.py:550
  195.6 4.8 %halve.9 = (bf16[2,2,192,768]{3,2,1,0:T(8,128)(2,1)}, f32[2,2,192,768]{3,2,1,0:T(8,128)}, bf16[1024,3072]{1,0:T(8,128)(2,1)}) custom-call(s32[1]{0:T(128)} %bitcast.3.me_ref, bf16[2,2,2,2,192,768]{5,4,3,2,1,0:T(8,128)(2,1)} %bitcast.142, bf16[2,2,2,192,768]{4,3,2,1,0:T(8,128)(2,1)} %bitcast.7.refs_1_, ...), custom_call_target="tpu_custom_call", output_to_operand_aliasing={{2}: (3, {})} | custom-call | tf_op jit(solution)/shard_map/halve/pallas_call | solution.py:738
  200.4 8.1 %convolution_convert_fusion = bf16[768,3072]{1,0:T(8,128)(2,1)S(1)} fusion(bf16[1024,768]{1,0:T(8,128)(2,1)S(1)} %copy-done.12, bf16[1024,3072]{1,0:T(8,128)(2,1)} %get-tuple-element.393.refs_32_), kind=kOutput, calls=%fused_computation | convolution fusion | flops 4834197504 | bytes 12582912 | tf_op jit(solution)/shard_map/dot_general | solution.py:45
  209.4 1.8 collective-permute-start.7
  211.2 2.3 collective-permute-done.5
  214.3 1.8 collective-permute-start.6
  218.6 17.2 %attn_back_0_1.1 = (bf16[1024,768]{1,0:T(8,128)(2,1)}, bf16[1024,2304]{1,0:T(8,128)(2,1)}, bf16[2,12,512,512]{3,2,1,0:T(8,128)(2,1)}, bf16[1024,768]{1,0:T(8,128...) custom-call(s32[1]{0:T(128)} %bitcast.refs_0_, ...), custom_call_target="tpu_custom_call", output_to_operand_aliasing={{0}: (18, {}), {1}: (19, {}), {2}: (20, {}), {3}: (21, {}),... | custom-call | tf_op jit(solution)/shard_map/attn_back_0_1/pallas_call | solution.py:550
  235.8 2.0 collective-permute-done.7
  237.7 3.0 halve.11
  240.7 5.0 %convolution_convert_fusion.2 = bf16[768,1536]{1,0:T(8,128)(2,1)S(1)} fusion(bf16[1024,768]{1,0:T(8,128)(2,1)} %get-tuple-element.421.refs_4_, bf16[1024,2304]{1,0:T(8,128)(2,1)} %get-tuple-element.422), kind=kOutput, calls=%fused_computation.2 | convolution fusion | flops 2417098752 | bytes 7077888 | tf_op jit(solution)/shard_map/dot_general | solution.py:45
  248.6 3.0 halve.12
  251.5 3.4 fusion.3
  256.3 2.7 collective-permute-start.18
  261.0 1.8 collective-permute-start.10
  264.8 20.8 %collective-permute-done.18 = bf16[2,192,768]{2,1,0:T(8,128)(2,1)S(1)} collective-permute-done((bf16[2,192,768]{2,1,0:T(8,128)(2,1)S(1)}, bf16[2,192,768]{2,1,0:T(8,128)(2,1)S(1)}, u32[]{:S(2)}, u32[]{:S(2)}) %collective-permute-start.18) | collective-permute-done | bytes 589856 | tf_op jit(solution)/shard_map/ppermute | solution.py:679
  287.4 3.0 collective-permute-done.12
  290.6 11.4 %collective-permute-done.11 = bf16[4,48,1536]{2,1,0:T(8,128)(2,1)S(1)} collective-permute-done((bf16[4,48,1536]{2,1,0:T(8,128)(2,1)S(1)}, bf16[4,48,1536]{2,1,0:T(8,128)(2,1)S(1)}, u32[]{:S(2)}, u32[]{:S(2)}) %collective-permute-start.11) | collective-permute-done | bytes 589856 | tf_op jit(solution)/shard_map/ppermute | solution.py:679
  302.5 5.2 %collective-permute-start.14 = (bf16[2,48,1536]{2,1,0:T(8,128)(2,1)S(1)}, bf16[2,48,1536]{2,1,0:T(8,128)(2,1)S(1)}, u32[]{:S(2)}, u32[]{:S(2)}) collective-permute-start(bf16[2,48,1536]{2,1,0:T(8,128)(2,1)S(1)} %bitcast.136), channel_id=1, source_target_pairs={{0,8},{1,9},{2,10},{3,11},{4,12},{5,13},{6,14},{7,15},{8,0},{9,1},... | collective-permute-start | bytes 884744 | tf_op jit(solution)/shard_map/ppermute | solution.py:679
  308.6 19.7 %collective-permute-done.14 = bf16[2,48,1536]{2,1,0:T(8,128)(2,1)S(1)} collective-permute-done((bf16[2,48,1536]{2,1,0:T(8,128)(2,1)S(1)}, bf16[2,48,1536]{2,1,0:T(8,128)(2,1)S(1)}, u32[]{:S(2)}, u32[]{:S(2)}) %collective-permute-start.14) | collective-permute-done | bytes 294944 | tf_op jit(solution)/shard_map/ppermute | solution.py:679
  329.0 8.6 %collective-permute-done.17 = bf16[1,48,3072]{2,1,0:T(8,128)(2,1)S(1)} collective-permute-done((bf16[1,48,3072]{2,1,0:T(8,128)(2,1)S(1)}, bf16[1,48,3072]{2,1,0:T(8,128)(2,1)S(1)}, u32[]{:S(2)}, u32[]{:S(2)}) %collective-permute-start.17) | collective-permute-done | bytes 294944 | tf_op jit(solution)/shard_map/ppermute | solution.py:679
  (86 shorter events, 30.8 us)
Async XLA Ops:
  26.6 28.1 %collective-permute-start.1 = (bf16[512,768]{1,0:T(8,128)(2,1)}, bf16[512,768]{1,0:T(8,128)(2,1)S(1)}, u32[]{:S(2)}, u32[]{:S(2)}) collective-permute-start(bf16[512,768]{1,0:T(8,128)(2,1)} %get-tuple-element.277), channel_id=1, source_target_pairs={{0,16},{1,17},{2,18},{3,19},{4,20},{5,21},{6,22},{7,23},{8,24},{9,... | collective-permute-start | bytes 2359304 | tf_op jit(solution)/shard_map/ppermute | solution.py:778
  53.3 19.3 %collective-permute-start = (bf16[512,768]{1,0:T(8,128)(2,1)}, bf16[512,768]{1,0:T(8,128)(2,1)S(1)}, u32[]{:S(2)}, u32[]{:S(2)}) collective-permute-start(bf16[512,768]{1,0:T(8,128)(2,1)} %get-tuple-element.276), channel_id=1, source_target_pairs={{0,16},{1,17},{2,18},{3,19},{4,20},{5,21},{6,22},{7,23},{8,24},{9,... | collective-permute-start | bytes 2359304 | tf_op jit(solution)/shard_map/ppermute | solution.py:778
  66.9 52.7 %collective-permute-start.3 = (bf16[512,768]{1,0:T(8,128)(2,1)}, bf16[512,768]{1,0:T(8,128)(2,1)S(1)}, u32[]{:S(2)}, u32[]{:S(2)}) collective-permute-start(bf16[512,768]{1,0:T(8,128)(2,1)} %get-tuple-element.323), channel_id=1, source_target_pairs={{16,0},{17,1},{18,2},{19,3},{20,4},{21,5},{22,6},{23,7},{24,8},{25... | collective-permute-start | bytes 2359304 | tf_op jit(solution)/shard_map/ppermute | solution.py:778
  75.4 88.5 %collective-permute-start.2 = (bf16[512,768]{1,0:T(8,128)(2,1)}, bf16[512,768]{1,0:T(8,128)(2,1)S(1)}, u32[]{:S(2)}, u32[]{:S(2)}) collective-permute-start(bf16[512,768]{1,0:T(8,128)(2,1)} %get-tuple-element.322), channel_id=1, source_target_pairs={{16,0},{17,1},{18,2},{19,3},{20,4},{21,5},{22,6},{23,7},{24,8},{25... | collective-permute-start | bytes 2359304 | tf_op jit(solution)/shard_map/ppermute | solution.py:778
  178.1 3.0 copy-start.14
  181.0 14.6 %collective-permute-start.4 = (bf16[8,192,768]{2,1,0:T(8,128)(2,1)}, bf16[8,192,768]{2,1,0:T(8,128)(2,1)}, u32[]{:S(2)}, u32[]{:S(2)}) collective-permute-start(bf16[8,192,768]{2,1,0:T(8,128)(2,1)} %dynamic-slice_bitcast_fusion.1.refs_16_), channel_id=1, source_target_pairs={{0,1},{1,0},{2,3},{3,2},{4,5},{5,4},{6,7},{7,6},{8,9},{9,8},{10,11... | collective-permute-start | bytes 7077896 | tf_op jit(solution)/shard_map/ppermute | solution.py:679
  195.6 4.8 %copy-start.12 = (bf16[1024,768]{1,0:T(8,128)(2,1)S(1)}, bf16[1024,768]{1,0:T(8,128)(2,1)}, u32[]{:S(2)}) copy-start(bf16[1024,768]{1,0:T(8,128)(2,1)} %get-tuple-element.392.refs_24_) | copy-start | bytes 4718596
  208.8 4.7 %collective-permute-start.5 = (bf16[8,48,3072]{2,1,0:T(8,128)(2,1)S(1)}, bf16[8,48,3072]{2,1,0:T(8,128)(2,1)S(1)}, u32[]{:S(2)}, u32[]{:S(2)}) collective-permute-start(bf16[8,48,3072]{2,1,0:T(8,128)(2,1)S(1)} %dynamic-slice_bitcast_fusion), channel_id=1, source_target_pairs={{0,1},{1,0},{2,3},{3,2},{4,5},{5,4},{6,7},{7,6},{8,9},{9,8},{10,11... | collective-permute-start | bytes 7077896 | tf_op jit(solution)/shard_map/ppermute | solution.py:679
  209.4 28.4 %collective-permute-start.7 = (bf16[4,192,768]{2,1,0:T(8,128)(2,1)}, bf16[4,192,768]{2,1,0:T(8,128)(2,1)}, u32[]{:S(2)}, u32[]{:S(2)}) collective-permute-start(bf16[4,192,768]{2,1,0:T(8,128)(2,1)} %bitcast.8.refs_16_), channel_id=1, source_target_pairs={{0,4},{1,5},{2,6},{3,7},{4,0},{5,1},{6,2},{7,3},{8,12},{9,13},{10,... | collective-permute-start | bytes 3538952 | tf_op jit(solution)/shard_map/ppermute | solution.py:679
  213.5 2.6 copy-start.11
  213.5 2.6 copy-start.13
  214.3 3.3 copy-start.5
  214.3 3.3 copy-start.8
  214.3 34.2 %collective-permute-start.6 = (bf16[4,48,3072]{2,1,0:T(8,128)(2,1)S(1)}, bf16[4,48,3072]{2,1,0:T(8,128)(2,1)}, u32[]{:S(2)}, u32[]{:S(2)}) collective-permute-start(bf16[4,48,3072]{2,1,0:T(8,128)(2,1)S(1)} %bitcast.103), channel_id=1, source_target_pairs={{0,2},{1,3},{2,0},{3,1},{4,6},{5,7},{6,4},{7,5},{8,10},{9,11},{10,... | collective-permute-start | bytes 3538952 | tf_op jit(solution)/shard_map/ppermute | solution.py:679
  245.8 2.7 copy-start.1
  251.5 3.5 %copy-start.15 = (bf16[8,48,768]{2,1,0:T(8,128)(2,1)S(1)}, bf16[8,48,768]{2,1,0:T(8,128)(2,1)}, u32[]{:S(2)}) copy-start(bf16[8,48,768]{2,1,0:T(8,128)(2,1)} %dynamic-slice_bitcast_fusion.4) | copy-start | bytes 1769476
  254.9 1.4 copy-start.20
  254.9 4.9 %copy-start.9 = (bf16[2,1,48,3072]{3,2,1,0:T(8,128)(2,1)S(1)}, bf16[2,1,48,3072]{3,2,1,0:T(8,128)(2,1)}, u32[]{:S(2)}) copy-start(bf16[2,1,48,3072]{3,2,1,0:T(8,128)(2,1)} %get-tuple-element.427) | copy-start | bytes 1769476
  255.1 4.7 %collective-permute-start.8 = (bf16[8,48,1664]{2,1,0:T(8,128)(2,1)S(1)}, bf16[8,48,1664]{2,1,0:T(8,128)(2,1)S(1)}, u32[]{:S(2)}, u32[]{:S(2)}) collective-permute-start(bf16[8,48,1664]{2,1,0:T(8,128)(2,1)S(1)} %pad_maximum_fusion), channel_id=1, source_target_pairs={{0,1},{1,0},{2,3},{3,2},{4,5},{5,4},{6,7},{7,6},{8,9},{9,8},{10,11... | collective-permute-start | bytes 3833864 | tf_op jit(solution)/shard_map/ppermute | solution.py:679
  256.2 3.7 %collective-permute-start.9 = (bf16[8,48,1536]{2,1,0:T(8,128)(2,1)S(1)}, bf16[8,48,1536]{2,1,0:T(8,128)(2,1)S(1)}, u32[]{:S(2)}, u32[]{:S(2)}) collective-permute-start(bf16[8,48,1536]{2,1,0:T(8,128)(2,1)S(1)} %copy-done.2), channel_id=1, source_target_pairs={{0,1},{1,0},{2,3},{3,2},{4,5},{5,4},{6,7},{7,6},{8,9},{9,8},{10,11... | collective-permute-start | bytes 3538952 | tf_op jit(solution)/shard_map/ppermute | solution.py:679
  256.3 29.3 %collective-permute-start.18 = (bf16[2,192,768]{2,1,0:T(8,128)(2,1)S(1)}, bf16[2,192,768]{2,1,0:T(8,128)(2,1)S(1)}, u32[]{:S(2)}, u32[]{:S(2)}) collective-permute-start(bf16[2,192,768]{2,1,0:T(8,128)(2,1)S(1)} %bitcast.145), channel_id=1, source_target_pairs={{0,8},{1,9},{2,10},{3,11},{4,12},{5,13},{6,14},{7,15},{8,0},{9,1},... | collective-permute-start | bytes 1769480 | tf_op jit(solution)/shard_map/ppermute | solution.py:679
  259.9 25.8 %copy-start.6 = (f32[1,2,192,768]{3,2,1,0:T(8,128)S(1)}, f32[1,2,192,768]{3,2,1,0:T(8,128)}, u32[]{:S(2)}) copy-start(f32[1,2,192,768]{3,2,1,0:T(8,128)} %get-tuple-element.448) | copy-start | bytes 3538948
  261.0 29.4 %copy-start.7 = (f32[2,1,48,3072]{3,2,1,0:T(8,128)S(1)}, f32[2,1,48,3072]{3,2,1,0:T(8,128)}, u32[]{:S(2)}) copy-start(f32[2,1,48,3072]{3,2,1,0:T(8,128)} %get-tuple-element.432) | copy-start | bytes 3538948
  261.0 40.9 %collective-permute-start.10 = (bf16[4,48,1664]{2,1,0:T(8,128)(2,1)S(1)}, bf16[4,48,1664]{2,1,0:T(8,128)(2,1)S(1)}, u32[]{:S(2)}, u32[]{:S(2)}) collective-permute-start(bf16[4,48,1664]{2,1,0:T(8,128)(2,1)S(1)} %bitcast.132), channel_id=1, source_target_pairs={{0,2},{1,3},{2,0},{3,1},{4,6},{5,7},{6,4},{7,5},{8,10},{9,11},{10,... | collective-permute-start | bytes 1916936 | tf_op jit(solution)/shard_map/ppermute | solution.py:679
  262.8 27.7 %collective-permute-start.12 = (bf16[2,48,3072]{2,1,0:T(8,128)(2,1)S(1)}, bf16[2,48,3072]{2,1,0:T(8,128)(2,1)S(1)}, u32[]{:S(2)}, u32[]{:S(2)}) collective-permute-start(bf16[2,48,3072]{2,1,0:T(8,128)(2,1)S(1)} %bitcast.108), channel_id=1, source_target_pairs={{0,4},{1,5},{2,6},{3,7},{4,0},{5,1},{6,2},{7,3},{8,12},{9,13},{10,... | collective-permute-start | bytes 1769480 | tf_op jit(solution)/shard_map/ppermute | solution.py:679
  264.4 37.6 %collective-permute-start.11 = (bf16[4,48,1536]{2,1,0:T(8,128)(2,1)S(1)}, bf16[4,48,1536]{2,1,0:T(8,128)(2,1)S(1)}, u32[]{:S(2)}, u32[]{:S(2)}) collective-permute-start(bf16[4,48,1536]{2,1,0:T(8,128)(2,1)S(1)} %bitcast.133), channel_id=1, source_target_pairs={{0,4},{1,5},{2,6},{3,7},{4,0},{5,1},{6,2},{7,3},{8,12},{9,13},{10,... | collective-permute-start | bytes 1769480 | tf_op jit(solution)/shard_map/ppermute | solution.py:679
  285.8 21.9 %collective-permute-start.19 = (bf16[1,192,768]{2,1,0:T(8,128)(2,1)S(1)}, bf16[1,192,768]{2,1,0:T(8,128)(2,1)S(1)}, u32[]{:S(2)}, u32[]{:S(2)}) collective-permute-start(bf16[1,192,768]{2,1,0:T(8,128)(2,1)S(1)} %bitcast.135), channel_id=1, source_target_pairs={{0,2},{1,3},{2,0},{3,1},{4,6},{5,7},{6,4},{7,5},{8,10},{9,11},{10,... | collective-permute-start | bytes 884744 | tf_op jit(solution)/shard_map/ppermute | solution.py:679
  302.4 25.9 %collective-permute-start.13 = (bf16[2,48,1664]{2,1,0:T(8,128)(2,1)S(1)}, bf16[2,48,1664]{2,1,0:T(8,128)(2,1)S(1)}, u32[]{:S(2)}, u32[]{:S(2)}) collective-permute-start(bf16[2,48,1664]{2,1,0:T(8,128)(2,1)S(1)} %bitcast.134), channel_id=1, source_target_pairs={{0,4},{1,5},{2,6},{3,7},{4,0},{5,1},{6,2},{7,3},{8,12},{9,13},{10,... | collective-permute-start | bytes 958472 | tf_op jit(solution)/shard_map/ppermute | solution.py:679
  302.5 25.8 %collective-permute-start.14 = (bf16[2,48,1536]{2,1,0:T(8,128)(2,1)S(1)}, bf16[2,48,1536]{2,1,0:T(8,128)(2,1)S(1)}, u32[]{:S(2)}, u32[]{:S(2)}) collective-permute-start(bf16[2,48,1536]{2,1,0:T(8,128)(2,1)S(1)} %bitcast.136), channel_id=1, source_target_pairs={{0,8},{1,9},{2,10},{3,11},{4,12},{5,13},{6,14},{7,15},{8,0},{9,1},... | collective-permute-start | bytes 884744 | tf_op jit(solution)/shard_map/ppermute | solution.py:679
  307.7 30.0 %collective-permute-start.17 = (bf16[1,48,3072]{2,1,0:T(8,128)(2,1)S(1)}, bf16[1,48,3072]{2,1,0:T(8,128)(2,1)S(1)}, u32[]{:S(2)}, u32[]{:S(2)}) collective-permute-start(bf16[1,48,3072]{2,1,0:T(8,128)(2,1)S(1)} %bitcast.126), channel_id=1, source_target_pairs={{0,8},{1,9},{2,10},{3,11},{4,12},{5,13},{6,14},{7,15},{8,0},{9,1},... | collective-permute-start | bytes 884744 | tf_op jit(solution)/shard_map/ppermute | solution.py:679
  328.4 11.0 %collective-permute-start.15 = (bf16[1,48,1664]{2,1,0:T(8,128)(2,1)S(1)}, bf16[1,48,1664]{2,1,0:T(8,128)(2,1)S(1)}, u32[]{:S(2)}, u32[]{:S(2)}) collective-permute-start(bf16[1,48,1664]{2,1,0:T(8,128)(2,1)S(1)} %bitcast.137), channel_id=1, source_target_pairs={{0,8},{1,9},{2,10},{3,11},{4,12},{5,13},{6,14},{7,15},{8,0},{9,1},... | collective-permute-start | bytes 479240 | tf_op jit(solution)/shard_map/ppermute | solution.py:679
  328.4 10.1 %collective-permute-start.16 = (bf16[1,48,1536]{2,1,0:T(8,128)(2,1)S(1)}, bf16[1,48,1536]{2,1,0:T(8,128)(2,1)S(1)}, u32[]{:S(2)}, u32[]{:S(2)}) collective-permute-start(bf16[1,48,1536]{2,1,0:T(8,128)(2,1)S(1)} %bitcast.138), channel_id=1, source_target_pairs={{0,2},{1,3},{2,0},{3,1},{4,6},{5,7},{6,4},{7,5},{8,10},{9,11},{10,... | collective-permute-start | bytes 442376 | tf_op jit(solution)/shard_map/ppermute | solution.py:679
  (9 other events, 10.0 us)
where the time goes:
time: 344 us; the launch traced here: 341 us
  Pallas kernels  148 us (43%)
  waiting for transfers between devices  128 us (37%)
  matrix products  25.7 us (7%)
  starting transfers between devices  23.8 us (7%)
  local copies, waits for them, and re-layouts  12.3 us (4%)
    pallas_call x9, Pallas kernels, layer_step(): pl.pallas_call(functools.partial(layer_kernel, work, phase_on, block, INS...  132 us
    ppermute x16, waiting for transfers between devices, swap(): lax.ppermute(theirs, 'dp', [(i, i ^ 1 << bit) for i in range(count)])  69.5 us
    ppermute x4, waiting for transfers between devices, passed_along(): return lax.ppermute(x, axis, pairs)  58.8 us
    dot_general x5, matrix products, dot_tn(): lax.dot_general(a, b, (((0,), (0,)), ((), ())), preferred_element_type=F32)  25.7 us
    ppermute x16, starting transfers between devices, swap(): lax.ppermute(theirs, 'dp', [(i, i ^ 1 << bit) for i in range(count)])  18.5 us
    pallas_call x9, Pallas kernels, halve_all(): pl.pallas_call(functools.partial(halve_kernel, tuple(bits), tuple(counts)...  13.4 us
    unnamed x44, local copies, waits for them, and re-layouts  9.22 us
  transfers between devices with their start and end apart: 20, of which 12 were waited for; matrix products, arithmetic and copies ran while one was open for 3% of the time, Pallas kernels for 32%

commit v1 on v0

--- a/solution.py
+++ b/solution.py
@@ -463,7 +463,7 @@
         self.norm_sums_2(block)
         self.attn_back(block)
 
-    def do_norm_back(self, block):
+    def do_ffn_back(self, block):
         rows = self.rows(block)
         loads = [
             self.copies.load(source, target)
@@ -473,18 +473,6 @@
                 (self.scale2.at[rows], self.scale2_v),
             )
         ]
-        for load in loads:
-            load.wait()
-        self.norm_back(block)
-        self.copies.store(self.acc_v, self.residual)
-        self.norm_sums_2(block)
-
-    def do_ffn_back(self, block):
-        rows = self.rows(block)
-        loads = [
-            self.copies.load(self.outer_low.at[rows], self.outer_v),
-            self.copies.load(self.residual, self.acc_v),
-        ]
         for i in range(min(2, self.stages)):
             for load in self.chunk_loads(i, rows):
                 load.start()
@@ -494,8 +482,10 @@
             self.copies.load(self.form1.at[rows], self.form1_v),
             self.copies.load(self.scale1.at[rows], self.scale1_v),
         ]
+        self.norm_back(block)
         self.ffn_back(block, True, middle)
         self.copies.store(self.acc_v, self.residual)
+        self.norm_sums_2(block)
 
     def do_attn_back(self, block):
         rows = self.rows(block)
@@ -542,9 +532,7 @@
     names = list(scratch)
     kept = list(kept) if kept is not None else []
     sent = jax.ShapeDtypeStruct((BLOCK, values[2].shape[1]), BF16)
-    if work == "norm_back":
-        names = [f"{name}_v" for name in ("g", "form2", "scale2", "acc", "outer", "sums2")]
-    elif work == "bias":
+    if work == "bias":
         names = ["values_v", "bias_v"]
     count = len(values) + len(afters)
     results = pl.pallas_call(
@@ -842,7 +830,7 @@
     kept, sent = step("both", 1, 1, second, kept)
     second_back = passed_along(sent, "phase", -1)
     kept, _ = step("back", 0, 0, first_back, kept)
-    kept, _ = step("norm_back", 0, 1, second_back, kept)
+    kept, _ = step("ffn_back", 0, 1, second_back, kept)
 
     bits = ways.bit_length() - 1
     near_first = list(range(bits))
@@ -853,24 +841,20 @@
         product = dot_tn(left, right).astype(BF16)
         return product.reshape(ways, product.shape[0] // ways, product.shape[1])
 
-    down = Share([weight_grad(kept["act"], kept["outer_low"])], far_first)
-    kept, _ = step("ffn_back", 0, 1, hidden_in, kept, [down.sent])
-    (hidden_low,) = halve_all(me, [down], through=[kept["hidden_low"]])
-    up = Share([weight_grad(kept["low1"], hidden_low)], near_first)
+    down = Share([weight_grad(kept["act"], kept["outer_low"])], near_first)
+    up = Share([weight_grad(kept["low1"], kept["hidden_low"])], far_first)
     out_part = weight_grad(kept["ctx"], kept["residual_low"])
-    kept["hidden_low"] = hidden_low
+    halve_all(me, [down])
     halve_all(me, [up])
     kept, _ = step("attn_back", 0, 1, hidden_in, kept, [down.sent, up.sent])
-    (projected,) = halve_all(me, [down], through=[kept["projected"]])
-    far = Share([weight_grad(kept["xin"], projected[:, width:])], far_first)
-    (slots_in,) = halve_all(me, [up], [down.sent, far.sent], [kept["xin"]])
-    near_part = weight_grad(slots_in, projected[:, :width])
+    far = Share([weight_grad(kept["xin"], kept["projected"][:, width:])], far_first)
+    (slots_in,) = halve_all(me, [down, up], [far.sent], [kept["xin"]])
+    near_part = weight_grad(slots_in, kept["projected"][:, :width])
     small = packed(ways, buckets, rel_buckets[None, :], kept, [far.sent])
     near = Share([out_part, near_part, small], near_first)
-    halve_all(me, [down])
-    halve_all(me, [near, far], [up.sent])
-    halve_all(me, [up])
-    halve_all(me, [near, far], [up.sent])
+    halve_all(me, [near, far], [down.sent, up.sent])
+    halve_all(me, [down, up])
+    halve_all(me, [near, far], [down.sent, up.sent])
     while down.order:
         halve_all(me, [down, up])
     while near.order:

time: 344 us -> 316 us (0.919)
  waiting for transfers between devices: 128 us -> 113 us
  Pallas kernels: 148 us -> 138 us
    ppermute x16, waiting for transfers between devices: 69.5 us -> 54.4 us  [swap(): lax.ppermute(theirs, 'dp', [(i, i ^ 1 << bit) for i in range(count)])]
    pallas_call x9 -> x8, Pallas kernels: 132 us -> 127 us  [layer_step(): pl.pallas_call(functools.partial(layer_kernel, work, phase_on, block, INS...]
    pallas_call x9 -> x7, Pallas kernels: 13.4 us -> 9.24 us  [halve_all(): pl.pallas_call(functools.partial(halve_kernel, tuple(bits), tuple(counts)...]
    unnamed x44 -> x46, local copies, waits for them, and re-layouts: 9.22 us -> 10.6 us
  transfers between devices with their start and end apart: 20 -> 20, of which waited for: 12 -> 11; matrix products, arithmetic and copies ran while one was open for 3% -> 5% of each run, Pallas kernels for 32% -> 30%
where the time goes in v1:
time: 316 us; the launch traced here: 314 us
  Pallas kernels  138 us (44%)
  waiting for transfers between devices  113 us (36%)
  starting transfers between devices  23.8 us (8%)
  matrix products  23.1 us (7%)
  local copies, waits for them, and re-layouts  11.9 us (4%)
    pallas_call x8, Pallas kernels, layer_step(): pl.pallas_call(functools.partial(layer_kernel, work, phase_on, block, INS...  127 us
    ppermute x4, waiting for transfers between devices, passed_along(): return lax.ppermute(x, axis, pairs)  58.8 us
    ppermute x16, waiting for transfers between devices, swap(): lax.ppermute(theirs, 'dp', [(i, i ^ 1 << bit) for i in range(count)])  54.4 us
    dot_general x5, matrix products, dot_tn(): lax.dot_general(a, b, (((0,), (0,)), ((), ())), preferred_element_type=F32)  23.1 us
    ppermute x16, starting transfers between devices, swap(): lax.ppermute(theirs, 'dp', [(i, i ^ 1 << bit) for i in range(count)])  18.6 us
    unnamed x46, local copies, waits for them, and re-layouts  10.6 us
    pallas_call x7, Pallas kernels, halve_all(): pl.pallas_call(functools.partial(halve_kernel, tuple(bits), tuple(counts)...  9.24 us
  transfers between devices with their start and end apart: 20, of which 11 were waited for; matrix products, arithmetic and copies ran while one was open for 5% of the time, Pallas kernels for 30%

profile of v1, /device:TPU:0, one launch (start us, length us, event | category | flops | bytes accessed | tf_op | source)
XLA Modules:
  0.0 313.6 jit_solution(3410454159352189528)
XLA Ops:
  0.6 1.5 copy.187.refs_5_
  2.1 24.4 %forward_0_0.1 = (bf16[1024,768]{1,0:T(8,128)(2,1)}, bf16[1024,2304]{1,0:T(8,128)(2,1)}, bf16[2,12,512,512]{3,2,1,0:T(8,128)(2,1)}, bf16[1024,768]{1,0:T(8,128)(...) custom-call(s32[1]{0:T(128)} %bitcast.refs_0_, ...), custom_call_target="tpu_custom_call" | custom-call | tf_op jit(solution)/shard_map/forward_0_0/pallas_call | solution.py:538
  27.9 1.8 bias_1_0.1
  29.7 23.6 %forward_0_1.1 = (bf16[1024,768]{1,0:T(8,128)(2,1)}, bf16[1024,2304]{1,0:T(8,128)(2,1)}, bf16[2,12,512,512]{3,2,1,0:T(8,128)(2,1)}, bf16[1024,768]{1,0:T(8,128)(...) custom-call(s32[1]{0:T(128)} %bitcast.refs_0_, ...), custom_call_target="tpu_custom_call", output_to_operand_aliasing={{0}: (16, {}), {1}: (17, {}), {2}: (18, {}), {3}: (19, {}),... | custom-call | tf_op jit(solution)/shard_map/forward_0_1/pallas_call | solution.py:538
  55.6 11.3 %both_1_0.1 = (bf16[1024,768]{1,0:T(8,128)(2,1)}, bf16[1024,2304]{1,0:T(8,128)(2,1)}, bf16[2,12,512,512]{3,2,1,0:T(8,128)(2,1)}, bf16[1024,768]{1,0:T(8,128)(2,1...) custom-call(s32[1]{0:T(128)} %bitcast.refs_0_, ...), custom_call_target="tpu_custom_call", output_to_operand_aliasing={{0}: (16, {}), {1}: (17, {}), {2}: (18, {}), {3}: (19, {}),... | custom-call | tf_op jit(solution)/shard_map/both_1_0/pallas_call | solution.py:538
  68.2 4.4 %collective-permute-done.refs_3_ = bf16[512,768]{1,0:T(8,128)(2,1)S(1)} collective-permute-done((bf16[512,768]{1,0:T(8,128)(2,1)}, bf16[512,768]{1,0:T(8,128)(2,1)S(1)}, u32[]{:S(2)}, u32[]{:S(2)}) %collective-permute-start) | collective-permute-done | bytes 786464 | tf_op jit(solution)/shard_map/ppermute | solution.py:766
  73.5 1.9 both_1_1.1
  76.7 42.9 %collective-permute-done.3.refs_3_ = bf16[512,768]{1,0:T(8,128)(2,1)S(1)} collective-permute-done((bf16[512,768]{1,0:T(8,128)(2,1)}, bf16[512,768]{1,0:T(8,128)(2,1)S(1)}, u32[]{:S(2)}, u32[]{:S(2)}) %collective-permute-start.3) | collective-permute-done | bytes 786464 | tf_op jit(solution)/shard_map/ppermute | solution.py:766
  120.5 32.0 %back_0_0.1 = (bf16[1024,768]{1,0:T(8,128)(2,1)}, bf16[1024,2304]{1,0:T(8,128)(2,1)}, bf16[2,12,512,512]{3,2,1,0:T(8,128)(2,1)}, bf16[1024,768]{1,0:T(8,128)(2,1...) custom-call(s32[1]{0:T(128)} %bitcast.refs_0_, ...), custom_call_target="tpu_custom_call", output_to_operand_aliasing={{0}: (16, {}), {1}: (17, {}), {2}: (18, {}), {3}: (19, {}),... | custom-call | tf_op jit(solution)/shard_map/back_0_0/pallas_call | solution.py:538
  152.4 11.5 %collective-permute-done.2.refs_3_ = bf16[512,768]{1,0:T(8,128)(2,1)S(1)} collective-permute-done((bf16[512,768]{1,0:T(8,128)(2,1)}, bf16[512,768]{1,0:T(8,128)(2,1)S(1)}, u32[]{:S(2)}, u32[]{:S(2)}) %collective-permute-start.2) | collective-permute-done | bytes 786464 | tf_op jit(solution)/shard_map/ppermute | solution.py:766
  164.9 14.5 %ffn_back_0_1.1 = (bf16[1024,768]{1,0:T(8,128)(2,1)}, bf16[1024,2304]{1,0:T(8,128)(2,1)}, bf16[2,12,512,512]{3,2,1,0:T(8,128)(2,1)}, bf16[1024,768]{1,0:T(8,128)...) custom-call(s32[1]{0:T(128)} %bitcast.refs_0_, ...), custom_call_target="tpu_custom_call", output_to_operand_aliasing={{0}: (16, {}), {1}: (17, {}), {2}: (18, {}), {3}: (19, {}),... | custom-call | tf_op jit(solution)/shard_map/ffn_back_0_1/pallas_call | solution.py:538
  179.4 7.8 %convolution_convert_fusion = bf16[768,3072]{1,0:T(8,128)(2,1)S(1)} fusion(bf16[1024,768]{1,0:T(8,128)(2,1)} %get-tuple-element.347.refs_24_, bf16[1024,3072]{1,0:T(8,128)(2,1)} %get-tuple-element.348.refs_32_), kind=kOutput, calls=%fused_computation | convolution fusion | flops 4834197504 | bytes 12582912 | tf_op jit(solution)/shard_map/dot_general | solution.py:45
  188.7 5.5 %convolution_convert_fusion.1 = bf16[3072,768]{1,0:T(8,128)(2,1)S(1)} fusion(bf16[1024,3072]{1,0:T(8,128)(2,1)S(1)} %copy-done.13, bf16[1024,768]{1,0:T(8,128)(2,1)S(1)} %copy-done.15), kind=kOutput, calls=%fused_computation.1 | convolution fusion | flops 4834197504 | bytes 12582912 | tf_op jit(solution)/shard_map/dot_general | solution.py:45
  195.5 1.4 copy-done.5
  196.9 1.8 collective-permute-start.7
  199.0 1.9 halve.7
  200.8 1.8 collective-permute-start.6
  202.6 1.4 convolution_convert_fusion.3
  204.9 17.2 %attn_back_0_1.1 = (bf16[1024,768]{1,0:T(8,128)(2,1)}, bf16[1024,2304]{1,0:T(8,128)(2,1)}, bf16[2,12,512,512]{3,2,1,0:T(8,128)(2,1)}, bf16[1024,768]{1,0:T(8,128...) custom-call(s32[1]{0:T(128)} %bitcast.refs_0_, ...), custom_call_target="tpu_custom_call", output_to_operand_aliasing={{0}: (18, {}), {1}: (19, {}), {2}: (20, {}), {3}: (21, {}),... | custom-call | tf_op jit(solution)/shard_map/attn_back_0_1/pallas_call | solution.py:538
  222.1 5.0 %convolution_convert_fusion.2 = bf16[768,1536]{1,0:T(8,128)(2,1)S(1)} fusion(bf16[1024,768]{1,0:T(8,128)(2,1)} %get-tuple-element.372.refs_5_, bf16[1024,2304]{1,0:T(8,128)(2,1)} %get-tuple-element.373), kind=kOutput, calls=%fused_computation.2 | convolution fusion | flops 2417098752 | bytes 7077888 | tf_op jit(solution)/shard_map/dot_general | solution.py:45
  228.4 1.5 pack.1
  230.0 4.4 %halve.9 = (bf16[2,1,192,768]{3,2,1,0:T(8,128)(2,1)}, f32[2,1,192,768]{3,2,1,0:T(8,128)}, bf16[1,2,48,3072]{3,2,1,0:T(8,128)(2,1)}, f32[1,2,48,3072]{3,2,1,0:T(8,128)}, bf16[1024,768]{1,0:T(8,128)(2,1)}) custom-call(s32[1]{0:T(128)} %bitcast.3.me_ref, f32[2,2,1,192,768]{4,3,2,1,0:T(8,128)} %bitcast.94, ...), custom_call_target="tpu_custom_call", output_to_operand_aliasing={{4}: (6, {})} | custom-call | tf_op jit(solution)/shard_map/halve/pallas_call | solution.py:726
  234.4 3.4 %fusion.3 = bf16[768,768]{1,0:T(8,128)(2,1)S(1)} fusion(bf16[1024,768]{1,0:T(8,128)(2,1)} %get-tuple-element.374, bf16[1024,2304]{1,0:T(8,128)(2,1)} %get-tuple-element.373), kind=kOutput, calls=%fused_computation.8 | convolution fusion | flops 1208549376 | bytes 4325376 | tf_op jit(solution)/shard_map/dot_general | solution.py:45
  239.2 1.6 collective-permute-start.12
  240.8 2.6 collective-permute-start.13
  246.5 21.5 %collective-permute-done.12 = bf16[2,192,768]{2,1,0:T(8,128)(2,1)S(1)} collective-permute-done((bf16[2,192,768]{2,1,0:T(8,128)(2,1)S(1)}, bf16[2,192,768]{2,1,0:T(8,128)(2,1)S(1)}, u32[]{:S(2)}, u32[]{:S(2)}) %collective-permute-start.12) | collective-permute-done | bytes 589856 | tf_op jit(solution)/shard_map/ppermute | solution.py:667
  271.7 14.7 %collective-permute-done.11 = bf16[4,48,1536]{2,1,0:T(8,128)(2,1)S(1)} collective-permute-done((bf16[4,48,1536]{2,1,0:T(8,128)(2,1)S(1)}, bf16[4,48,1536]{2,1,0:T(8,128)(2,1)S(1)}, u32[]{:S(2)}, u32[]{:S(2)}) %collective-permute-start.11) | collective-permute-done | bytes 589856 | tf_op jit(solution)/shard_map/ppermute | solution.py:667
  286.9 4.1 %collective-permute-start.15 = (bf16[2,48,1536]{2,1,0:T(8,128)(2,1)S(1)}, bf16[2,48,1536]{2,1,0:T(8,128)(2,1)S(1)}, u32[]{:S(2)}, u32[]{:S(2)}) collective-permute-start(bf16[2,48,1536]{2,1,0:T(8,128)(2,1)S(1)} %bitcast.140), channel_id=1, source_target_pairs={{0,8},{1,9},{2,10},{3,11},{4,12},{5,13},{6,14},{7,15},{8,0},{9,1},... | collective-permute-start | bytes 884744 | tf_op jit(solution)/shard_map/ppermute | solution.py:667
  291.9 8.1 %collective-permute-done.15 = bf16[2,48,1536]{2,1,0:T(8,128)(2,1)S(1)} collective-permute-done((bf16[2,48,1536]{2,1,0:T(8,128)(2,1)S(1)}, bf16[2,48,1536]{2,1,0:T(8,128)(2,1)S(1)}, u32[]{:S(2)}, u32[]{:S(2)}) %collective-permute-start.15) | collective-permute-done | bytes 294944 | tf_op jit(solution)/shard_map/ppermute | solution.py:667
  300.1 2.2 collective-permute-done.14
  305.5 3.3 %collective-permute-done.17 = bf16[1,48,1536]{2,1,0:T(8,128)(2,1)S(1)} collective-permute-done((bf16[1,48,1536]{2,1,0:T(8,128)(2,1)S(1)}, bf16[1,48,1536]{2,1,0:T(8,128)(2,1)S(1)}, u32[]{:S(2)}, u32[]{:S(2)}) %collective-permute-start.17) | collective-permute-done | bytes 147488 | tf_op jit(solution)/shard_map/ppermute | solution.py:667
  308.9 3.0 collective-permute-done.16
  (85 shorter events, 28.3 us)
Async XLA Ops:
  26.6 28.1 %collective-permute-start.1 = (bf16[512,768]{1,0:T(8,128)(2,1)}, bf16[512,768]{1,0:T(8,128)(2,1)S(1)}, u32[]{:S(2)}, u32[]{:S(2)}) collective-permute-start(bf16[512,768]{1,0:T(8,128)(2,1)} %get-tuple-element.253), channel_id=1, source_target_pairs={{0,16},{1,17},{2,18},{3,19},{4,20},{5,21},{6,22},{7,23},{8,24},{9,... | collective-permute-start | bytes 2359304 | tf_op jit(solution)/shard_map/ppermute | solution.py:766
  53.3 19.3 %collective-permute-start = (bf16[512,768]{1,0:T(8,128)(2,1)}, bf16[512,768]{1,0:T(8,128)(2,1)S(1)}, u32[]{:S(2)}, u32[]{:S(2)}) collective-permute-start(bf16[512,768]{1,0:T(8,128)(2,1)} %get-tuple-element.252), channel_id=1, source_target_pairs={{0,16},{1,17},{2,18},{3,19},{4,20},{5,21},{6,22},{7,23},{8,24},{9,... | collective-permute-start | bytes 2359304 | tf_op jit(solution)/shard_map/ppermute | solution.py:766
  66.9 52.7 %collective-permute-start.3 = (bf16[512,768]{1,0:T(8,128)(2,1)}, bf16[512,768]{1,0:T(8,128)(2,1)S(1)}, u32[]{:S(2)}, u32[]{:S(2)}) collective-permute-start(bf16[512,768]{1,0:T(8,128)(2,1)} %get-tuple-element.299), channel_id=1, source_target_pairs={{16,0},{17,1},{18,2},{19,3},{20,4},{21,5},{22,6},{23,7},{24,8},{25... | collective-permute-start | bytes 2359304 | tf_op jit(solution)/shard_map/ppermute | solution.py:766
  75.4 88.6 %collective-permute-start.2 = (bf16[512,768]{1,0:T(8,128)(2,1)}, bf16[512,768]{1,0:T(8,128)(2,1)S(1)}, u32[]{:S(2)}, u32[]{:S(2)}) collective-permute-start(bf16[512,768]{1,0:T(8,128)(2,1)} %get-tuple-element.298), channel_id=1, source_target_pairs={{16,0},{17,1},{18,2},{19,3},{20,4},{21,5},{22,6},{23,7},{24,8},{25... | collective-permute-start | bytes 2359304 | tf_op jit(solution)/shard_map/ppermute | solution.py:766
  179.4 8.1 %copy-start.13 = (bf16[1024,3072]{1,0:T(8,128)(2,1)S(1)}, bf16[1024,3072]{1,0:T(8,128)(2,1)}, u32[]{:S(2)}) copy-start(bf16[1024,3072]{1,0:T(8,128)(2,1)} %get-tuple-element.344.refs_26_) | copy-start | bytes 18874372
  187.3 1.4 copy-start.15
  187.4 7.0 %collective-permute-start.5 = (bf16[8,48,3072]{2,1,0:T(8,128)(2,1)S(1)}, bf16[8,48,3072]{2,1,0:T(8,128)(2,1)S(1)}, u32[]{:S(2)}, u32[]{:S(2)}) collective-permute-start(bf16[8,48,3072]{2,1,0:T(8,128)(2,1)S(1)} %dynamic-slice_bitcast_fusion), channel_id=1, source_target_pairs={{0,1},{1,0},{2,3},{3,2},{4,5},{5,4},{6,7},{7,6},{8,9},{9,8},{10,11... | collective-permute-start | bytes 7077896 | tf_op jit(solution)/shard_map/ppermute | solution.py:667
  194.3 4.6 %collective-permute-start.4 = (bf16[8,192,768]{2,1,0:T(8,128)(2,1)S(1)}, bf16[8,192,768]{2,1,0:T(8,128)(2,1)S(1)}, u32[]{:S(2)}, u32[]{:S(2)}) collective-permute-start(bf16[8,192,768]{2,1,0:T(8,128)(2,1)S(1)} %dynamic-slice_bitcast_fusion.1), channel_id=1, source_target_pairs={{0,1},{1,0},{2,3},{3,2},{4,5},{5,4},{6,7},{7,6},{8,9},{9,8},{10,11... | collective-permute-start | bytes 7077896 | tf_op jit(solution)/shard_map/ppermute | solution.py:667
  196.9 3.9 %copy-start.9 = (bf16[2,2,48,3072]{3,2,1,0:T(8,128)(2,1)}, bf16[2,2,48,3072]{3,2,1,0:T(8,128)(2,1)S(1)}, u32[]{:S(2)}) copy-start(bf16[2,2,48,3072]{3,2,1,0:T(8,128)(2,1)S(1)} %get-tuple-element.349) | copy-start | bytes 3538948
  196.9 33.1 %collective-permute-start.7 = (bf16[4,48,3072]{2,1,0:T(8,128)(2,1)S(1)}, bf16[4,48,3072]{2,1,0:T(8,128)(2,1)}, u32[]{:S(2)}, u32[]{:S(2)}) collective-permute-start(bf16[4,48,3072]{2,1,0:T(8,128)(2,1)S(1)} %bitcast.105), channel_id=1, source_target_pairs={{0,4},{1,5},{2,6},{3,7},{4,0},{5,1},{6,2},{7,3},{8,12},{9,13},{10,... | collective-permute-start | bytes 3538952 | tf_op jit(solution)/shard_map/ppermute | solution.py:667
  198.9 3.6 %copy-start.14 = (bf16[1024,768]{1,0:T(8,128)(2,1)S(1)}, bf16[1024,768]{1,0:T(8,128)(2,1)}, u32[]{:S(2)}) copy-start(bf16[1024,768]{1,0:T(8,128)(2,1)} %get-tuple-element.353.refs_21_) | copy-start | bytes 4718596
  199.0 3.6 %copy-start.16 = (bf16[1024,768]{1,0:T(8,128)(2,1)S(1)}, bf16[1024,768]{1,0:T(8,128)(2,1)}, u32[]{:S(2)}) copy-start(bf16[1024,768]{1,0:T(8,128)(2,1)} %get-tuple-element.361.refs_33_) | copy-start | bytes 4718596
  200.8 3.2 %copy-start.6 = (f32[4,1,192,768]{3,2,1,0:T(8,128)}, f32[4,1,192,768]{3,2,1,0:T(8,128)S(1)}, u32[]{:S(2)}) copy-start(f32[4,1,192,768]{3,2,1,0:T(8,128)S(1)} %get-tuple-element.370) | copy-start | bytes 7077892
  200.8 29.1 %collective-permute-start.6 = (bf16[4,192,768]{2,1,0:T(8,128)(2,1)}, bf16[4,192,768]{2,1,0:T(8,128)(2,1)}, u32[]{:S(2)}, u32[]{:S(2)}) collective-permute-start(bf16[4,192,768]{2,1,0:T(8,128)(2,1)} %bitcast.8.refs_16_), channel_id=1, source_target_pairs={{0,2},{1,3},{2,0},{3,1},{4,6},{5,7},{6,4},{7,5},{8,10},{9,11},{10,... | collective-permute-start | bytes 3538952 | tf_op jit(solution)/shard_map/ppermute | solution.py:667
  227.3 2.7 copy-start.1
  234.4 3.5 %copy-start.17 = (bf16[8,48,768]{2,1,0:T(8,128)(2,1)S(1)}, bf16[8,48,768]{2,1,0:T(8,128)(2,1)}, u32[]{:S(2)}) copy-start(bf16[8,48,768]{2,1,0:T(8,128)(2,1)} %dynamic-slice_bitcast_fusion.4) | copy-start | bytes 1769476
  237.8 1.4 copy-start.11
  237.8 3.0 copy-start.10
  238.0 5.4 %collective-permute-start.8 = (bf16[8,48,1664]{2,1,0:T(8,128)(2,1)S(1)}, bf16[8,48,1664]{2,1,0:T(8,128)(2,1)S(1)}, u32[]{:S(2)}, u32[]{:S(2)}) collective-permute-start(bf16[8,48,1664]{2,1,0:T(8,128)(2,1)S(1)} %pad_maximum_fusion), channel_id=1, source_target_pairs={{0,1},{1,0},{2,3},{3,2},{4,5},{5,4},{6,7},{7,6},{8,9},{9,8},{10,11... | collective-permute-start | bytes 3833864 | tf_op jit(solution)/shard_map/ppermute | solution.py:667
  239.1 4.3 %collective-permute-start.9 = (bf16[8,48,1536]{2,1,0:T(8,128)(2,1)S(1)}, bf16[8,48,1536]{2,1,0:T(8,128)(2,1)S(1)}, u32[]{:S(2)}, u32[]{:S(2)}) collective-permute-start(bf16[8,48,1536]{2,1,0:T(8,128)(2,1)S(1)} %copy-done.2), channel_id=1, source_target_pairs={{0,1},{1,0},{2,3},{3,2},{4,5},{5,4},{6,7},{7,6},{8,9},{9,8},{10,11... | collective-permute-start | bytes 3538952 | tf_op jit(solution)/shard_map/ppermute | solution.py:667
  239.2 28.7 %collective-permute-start.12 = (bf16[2,192,768]{2,1,0:T(8,128)(2,1)S(1)}, bf16[2,192,768]{2,1,0:T(8,128)(2,1)S(1)}, u32[]{:S(2)}, u32[]{:S(2)}) collective-permute-start(bf16[2,192,768]{2,1,0:T(8,128)(2,1)S(1)} %bitcast.111), channel_id=1, source_target_pairs={{0,4},{1,5},{2,6},{3,7},{4,0},{5,1},{6,2},{7,3},{8,12},{9,13},{10,... | collective-permute-start | bytes 1769480 | tf_op jit(solution)/shard_map/ppermute | solution.py:667
  240.8 28.5 %collective-permute-start.13 = (bf16[2,48,3072]{2,1,0:T(8,128)(2,1)S(1)}, bf16[2,48,3072]{2,1,0:T(8,128)(2,1)S(1)}, u32[]{:S(2)}, u32[]{:S(2)}) collective-permute-start(bf16[2,48,3072]{2,1,0:T(8,128)(2,1)S(1)} %bitcast.109), channel_id=1, source_target_pairs={{0,8},{1,9},{2,10},{3,11},{4,12},{5,13},{6,14},{7,15},{8,0},{9,1},... | collective-permute-start | bytes 1769480 | tf_op jit(solution)/shard_map/ppermute | solution.py:667
  243.4 25.9 %copy-start.7 = (f32[2,1,192,768]{3,2,1,0:T(8,128)S(1)}, f32[2,1,192,768]{3,2,1,0:T(8,128)}, u32[]{:S(2)}) copy-start(f32[2,1,192,768]{3,2,1,0:T(8,128)} %get-tuple-element.384) | copy-start | bytes 3538948
  243.4 25.9 %copy-start.8 = (f32[1,2,48,3072]{3,2,1,0:T(8,128)S(1)}, f32[1,2,48,3072]{3,2,1,0:T(8,128)}, u32[]{:S(2)}) copy-start(f32[1,2,48,3072]{3,2,1,0:T(8,128)} %get-tuple-element.385) | copy-start | bytes 3538948
  244.6 41.9 %collective-permute-start.10 = (bf16[4,48,1664]{2,1,0:T(8,128)(2,1)S(1)}, bf16[4,48,1664]{2,1,0:T(8,128)(2,1)S(1)}, u32[]{:S(2)}, u32[]{:S(2)}) collective-permute-start(bf16[4,48,1664]{2,1,0:T(8,128)(2,1)S(1)} %bitcast.137), channel_id=1, source_target_pairs={{0,2},{1,3},{2,0},{3,1},{4,6},{5,7},{6,4},{7,5},{8,10},{9,11},{10,... | collective-permute-start | bytes 1916936 | tf_op jit(solution)/shard_map/ppermute | solution.py:667
  245.6 40.9 %collective-permute-start.11 = (bf16[4,48,1536]{2,1,0:T(8,128)(2,1)S(1)}, bf16[4,48,1536]{2,1,0:T(8,128)(2,1)S(1)}, u32[]{:S(2)}, u32[]{:S(2)}) collective-permute-start(bf16[4,48,1536]{2,1,0:T(8,128)(2,1)S(1)} %bitcast.138), channel_id=1, source_target_pairs={{0,4},{1,5},{2,6},{3,7},{4,0},{5,1},{6,2},{7,3},{8,12},{9,13},{10,... | collective-permute-start | bytes 1769480 | tf_op jit(solution)/shard_map/ppermute | solution.py:667
  269.5 21.6 %collective-permute-start.18 = (bf16[1,48,3072]{2,1,0:T(8,128)(2,1)S(1)}, bf16[1,48,3072]{2,1,0:T(8,128)(2,1)S(1)}, u32[]{:S(2)}, u32[]{:S(2)}) collective-permute-start(bf16[1,48,3072]{2,1,0:T(8,128)(2,1)S(1)} %bitcast.130), channel_id=1, source_target_pairs={{0,2},{1,3},{2,0},{3,1},{4,6},{5,7},{6,4},{7,5},{8,10},{9,11},{10,... | collective-permute-start | bytes 884744 | tf_op jit(solution)/shard_map/ppermute | solution.py:667
  270.5 34.2 %collective-permute-start.19 = (bf16[1,192,768]{2,1,0:T(8,128)(2,1)S(1)}, bf16[1,192,768]{2,1,0:T(8,128)(2,1)S(1)}, u32[]{:S(2)}, u32[]{:S(2)}) collective-permute-start(bf16[1,192,768]{2,1,0:T(8,128)(2,1)S(1)} %bitcast.128), channel_id=1, source_target_pairs={{0,8},{1,9},{2,10},{3,11},{4,12},{5,13},{6,14},{7,15},{8,0},{9,1},... | collective-permute-start | bytes 884744 | tf_op jit(solution)/shard_map/ppermute | solution.py:667
  286.9 15.4 %collective-permute-start.14 = (bf16[2,48,1664]{2,1,0:T(8,128)(2,1)S(1)}, bf16[2,48,1664]{2,1,0:T(8,128)(2,1)S(1)}, u32[]{:S(2)}, u32[]{:S(2)}) collective-permute-start(bf16[2,48,1664]{2,1,0:T(8,128)(2,1)S(1)} %bitcast.139), channel_id=1, source_target_pairs={{0,4},{1,5},{2,6},{3,7},{4,0},{5,1},{6,2},{7,3},{8,12},{9,13},{10,... | collective-permute-start | bytes 958472 | tf_op jit(solution)/shard_map/ppermute | solution.py:667
  286.9 13.1 %collective-permute-start.15 = (bf16[2,48,1536]{2,1,0:T(8,128)(2,1)S(1)}, bf16[2,48,1536]{2,1,0:T(8,128)(2,1)S(1)}, u32[]{:S(2)}, u32[]{:S(2)}) collective-permute-start(bf16[2,48,1536]{2,1,0:T(8,128)(2,1)S(1)} %bitcast.140), channel_id=1, source_target_pairs={{0,8},{1,9},{2,10},{3,11},{4,12},{5,13},{6,14},{7,15},{8,0},{9,1},... | collective-permute-start | bytes 884744 | tf_op jit(solution)/shard_map/ppermute | solution.py:667
  302.4 9.5 %collective-permute-start.16 = (bf16[1,48,1664]{2,1,0:T(8,128)(2,1)S(1)}, bf16[1,48,1664]{2,1,0:T(8,128)(2,1)S(1)}, u32[]{:S(2)}, u32[]{:S(2)}) collective-permute-start(bf16[1,48,1664]{2,1,0:T(8,128)(2,1)S(1)} %bitcast.141), channel_id=1, source_target_pairs={{0,8},{1,9},{2,10},{3,11},{4,12},{5,13},{6,14},{7,15},{8,0},{9,1},... | collective-permute-start | bytes 479240 | tf_op jit(solution)/shard_map/ppermute | solution.py:667
  303.7 5.1 %collective-permute-start.17 = (bf16[1,48,1536]{2,1,0:T(8,128)(2,1)S(1)}, bf16[1,48,1536]{2,1,0:T(8,128)(2,1)S(1)}, u32[]{:S(2)}, u32[]{:S(2)}) collective-permute-start(bf16[1,48,1536]{2,1,0:T(8,128)(2,1)S(1)} %bitcast.142), channel_id=1, source_target_pairs={{0,2},{1,3},{2,0},{3,1},{4,6},{5,7},{6,4},{7,5},{8,10},{9,11},{10,... | collective-permute-start | bytes 442376 | tf_op jit(solution)/shard_map/ppermute | solution.py:667
  (10 other events, 11.4 us)

commit v2 on v1

--- a/solution.py
+++ b/solution.py
@@ -126,10 +126,11 @@
 
     def build_bias(self):
         span = self.buckets.shape[1]
-        bucket_ids = lax.broadcasted_iota(jnp.int32, (self.table.shape[1], span), 0)
+        bucket_ids = lax.broadcasted_iota(jnp.int32, (self.table.shape[2], span), 0)
         hot = (bucket_ids == self.buckets[...]).astype(F32)
+        table = jnp.concatenate([self.table[head] for head in range(self.table.shape[0])], 0)
         values = lax.dot_general(
-            self.table[0], hot, (((0,), (0,)), ((), ())), precision=highest, preferred_element_type=F32
+            table, hot, (((1,), (0,)), ((), ())), precision=highest, preferred_element_type=F32
         )
         self.values_v[:, :span] = values
         self.values_v[:, span:] = jnp.zeros((values.shape[0], SPAN - span), F32)
@@ -165,9 +166,8 @@
 
         for i, c in enumerate(range(0, 3 * width, width)):
             loads[i].wait()
-            if i == 2 and built:
-                for pair in range(self.pairs):
-                    load_bias(pair).start()
+            if built and i < 2:
+                load_bias(i).start()
             self.qkv_v[:, c : c + width] = dot_nn(self.x_v[...], self.wqkv_v[:, c : c + width]).astype(BF16)
         copies.store(self.x_v, self.xin.at[rows])
         copies.store(self.qkv_v, self.qkv.at[rows], keep)
@@ -213,7 +213,11 @@
             if built:
                 load_bias(pair).wait()
 
-            @pl.when(pair == 0)
+                @pl.when(pair + 2 < self.pairs)
+                def _():
+                    load_bias(pair + 2).start()
+
+            @pl.when(pair == 1)
             def _():
                 for load in later_loads:
                     load.start()
@@ -357,7 +361,7 @@
         copies.store(self.residual_low_v, self.residual_low.at[rows])
         copies.store(self.sums1_v, self.sums1.at[block])
 
-    def attn_back(self, block, load_pair=None, load_in=()):
+    def attn_back(self, block, next_loads=None, load_in=()):
         copies = self.copies
         rows = self.rows(block)
         self.dctx_v[...] = dot_nt(self.residual_low_v[...], self.wout_v[...]).astype(BF16)
@@ -367,11 +371,11 @@
             def lanes_of(part):
                 return self.lanes_of(pair, part)
 
+            if next_loads is not None:
+                next_loads(pair)
             q_pair, k_pair, v_pair = (self.qkv_v[:, lanes_of(part)] for part in range(3))
             grad_pair = self.dctx_v[:, lanes_of(0)]
             crossed = grad_pair.astype(F32) * self.ctx_v[:, lanes_of(0)].astype(F32)
-            if load_pair is not None:
-                load_pair(pair).wait()
             masks = [half_mask(which, k_pair.shape) for which in range(2)]
 
             def own(both, which):
@@ -473,11 +477,11 @@
                 (self.scale2.at[rows], self.scale2_v),
             )
         ]
-        for i in range(min(2, self.stages)):
-            for load in self.chunk_loads(i, rows):
-                load.start()
+        self.chunk_loads(0, rows)[0].start()
         for load in loads:
             load.wait()
+        for load in self.chunk_loads(0, rows)[1:] + self.chunk_loads(1, rows):
+            load.start()
         middle = [
             self.copies.load(self.form1.at[rows], self.form1_v),
             self.copies.load(self.scale1.at[rows], self.scale1_v),
@@ -491,29 +495,47 @@
         rows = self.rows(block)
         loads = [
             self.copies.load(source, target)
-            for source, target in (
-                (self.residual_low.at[rows], self.residual_low_v),
-                (self.wout.at[0], self.wout_v),
-                (self.qkv.at[rows], self.qkv_v),
-                (self.ctx.at[rows], self.ctx_v),
-            )
-        ]
-
-        def load_pair(pair):
+            for source, target in ((self.residual_low.at[rows], self.residual_low_v), (self.wout.at[0], self.wout_v))
+        ]
+        first = self.copies.take(5 * self.pairs)
+
+        def pair_loads(pair):
             heads = pl.ds(2 * pair, 2)
-            return pltpu.make_async_copy(
-                self.weights.at[block, heads], self.weights_v.at[heads], self.sems.at[self.pair_sems + pair]
-            )
-
-        for pair in range(self.pairs):
-            load_pair(pair).start()
+            sources = [(self.weights.at[block, heads], self.weights_v.at[heads])]
+            for source, target, parts in ((self.qkv, self.qkv_v, 3), (self.ctx, self.ctx_v, 1)):
+                for part in range(parts):
+                    lanes = self.lanes_of(pair, part)
+                    sources.append((source.at[rows, lanes], target.at[:, lanes]))
+            return [
+                pltpu.make_async_copy(source, target, self.sems.at[first + 5 * pair + k])
+                for k, (source, target) in enumerate(sources)
+            ]
+
+        for pair in range(2):
+            for load in pair_loads(pair):
+                load.start()
         for load in loads:
             load.wait()
         last = [
-            self.copies.load(self.wqkv.at[0], self.wqkv_v),
-            self.copies.load(self.residual, self.acc_v),
-        ]
-        self.attn_back(block, load_pair, last)
+            pltpu.make_async_copy(source, target, self.sems.at[self.copies.take()])
+            for source, target in ((self.wqkv.at[0], self.wqkv_v), (self.residual, self.acc_v))
+        ]
+
+        def next_loads(pair):
+            for load in pair_loads(pair):
+                load.wait()
+
+            @pl.when(pair + 2 < self.pairs)
+            def _():
+                for load in pair_loads(pair + 2):
+                    load.start()
+
+            @pl.when(pair == self.pairs - 3)
+            def _():
+                for load in last:
+                    load.start()
+
+        self.attn_back(block, next_loads, last)
 
 
 def layer_kernel(work, phase_on, block, ins, outs, scratch, after_count, kept_count, *refs):
@@ -542,7 +564,7 @@
         out_shape=list(kept_shapes) + [sent],
         in_specs=specs + [ANY] * (len(afters) + len(kept)),
         out_specs=[ANY] * (len(kept_shapes) + 1),
-        scratch_shapes=[pltpu.VMEM(*scratch[name]) for name in names] + [pltpu.SemaphoreType.DMA((80,))],
+        scratch_shapes=[pltpu.VMEM(*scratch[name]) for name in names] + [pltpu.SemaphoreType.DMA((96,))],
         input_output_aliases={count + i: i for i in range(len(kept))},
         compiler_params=pltpu.CompilerParams(vmem_limit_bytes=VMEM_BYTES),
         name=f"{work}_{phase_on}_{block}",
@@ -624,19 +646,18 @@
         rest_ref[0, 0] = total(mine)
 
 
-def join_kernel(kept_near, arrived_near, kept_far, arrived_far, out_ref, qkv_ref, table_ref, *refs):
+def join_kernel(kept_ref, arrived_ref, out_ref, qkv_ref, table_ref, *refs):
     norm_refs, turn_v = refs[:-1], refs[-1]
-    near = kept_near[...] + arrived_near[...].astype(F32)
+    total = kept_ref[...] + arrived_ref[...].astype(F32)
     wide = out_ref.shape[1]
-    share = qkv_ref.shape[1] - kept_far.shape[1]
-    out_ref[...] = near[:, :wide]
-    qkv_ref[:, :share] = near[:, wide : wide + share]
-    qkv_ref[:, share:] = kept_far[...] + arrived_far[...].astype(F32)
-    small = near[:, wide + share :]
-    table_ref[...] = small[: table_ref.shape[0], : table_ref.shape[1]]
+    out_ref[...] = total[:, :wide]
+    qkv_ref[...] = total[:, wide : 4 * wide]
+    small = total[:, 4 * wide :]
     turn_v[...] = jnp.zeros(turn_v.shape, F32)
     turn_v[: small.shape[0], :] = small
     turned = turn_v[...].T
+    for head in range(table_ref.shape[0]):
+        table_ref[head] = turned[head : head + 1, : table_ref.shape[2]]
     for i, ref in enumerate(norm_refs):
         ref[...] = turned[NORM_LANE + i : NORM_LANE + i + 1, : ref.shape[1]]
 
@@ -745,19 +766,17 @@
     return results[len(outs) :]
 
 
-def joined(near, far, width, table_shape):
-    parts = [x[0] for share in (near, far) for x in (share.mine, share.arrived)]
-    shapes = [(near.depth, width), (near.depth, near.wide + far.wide - width - LANES), table_shape]
-    shapes += [(1, near.depth)] * 4
+def joined(share, width, table_shape):
+    shapes = [(share.depth, width), (share.depth, 3 * width), table_shape] + [(1, share.depth)] * 4
     return pl.pallas_call(
         join_kernel,
         out_shape=[jax.ShapeDtypeStruct(dims, F32) for dims in shapes],
-        in_specs=[VMEM] * len(parts),
+        in_specs=[VMEM] * 2,
         out_specs=[VMEM] * len(shapes),
         scratch_shapes=[pltpu.VMEM((LANES, LANES), F32)],
         compiler_params=pltpu.CompilerParams(vmem_limit_bytes=SMALL_VMEM_BYTES),
         name="join",
-    )(*parts)
+    )(share.mine[0], share.arrived[0])
 
 
 def passed_along(x, axis, by):
@@ -814,7 +833,7 @@
 
     def step(work, phase_on, block, received, kept, afters=()):
         values = (
-            phase, seg_ids, hidden_in, received, out_grad, rel_table, pad_mask[None, :], rel_buckets[None, :],
+            phase, seg_ids, hidden_in, received, out_grad, rel_table.transpose(2, 0, 1), pad_mask[None, :], rel_buckets[None, :],
             norm1_gain, norm1_bias, norm2_gain, norm2_bias, qkv_weight, out_weight, up_weight, down_weight,
         )
         in_place = None if kept is None else [kept[name] for name in KEPT]
@@ -847,27 +866,27 @@
     halve_all(me, [down])
     halve_all(me, [up])
     kept, _ = step("attn_back", 0, 1, hidden_in, kept, [down.sent, up.sent])
-    far = Share([weight_grad(kept["xin"], kept["projected"][:, width:])], far_first)
-    (slots_in,) = halve_all(me, [down, up], [far.sent], [kept["xin"]])
-    near_part = weight_grad(slots_in, kept["projected"][:, :width])
-    small = packed(ways, buckets, rel_buckets[None, :], kept, [far.sent])
-    near = Share([out_part, near_part, small], near_first)
-    halve_all(me, [near, far], [down.sent, up.sent])
+    parts = [weight_grad(kept["xin"], kept["projected"][:, width:])]
+    (slots_in,) = halve_all(me, [down, up], [parts[0]], [kept["xin"]])
+    parts.append(weight_grad(slots_in, kept["projected"][:, :width]))
+    small = packed(ways, buckets, rel_buckets[None, :], kept, [])
+    last = Share([out_part, parts[1], parts[0], small], near_first)
+    halve_all(me, [last], [down.sent, up.sent])
     halve_all(me, [down, up])
-    halve_all(me, [near, far], [down.sent, up.sent])
+    halve_all(me, [last], [down.sent, up.sent])
     while down.order:
         halve_all(me, [down, up])
-    while near.order:
-        halve_all(me, [near, far])
+    while last.order:
+        halve_all(me, [last])
     down_share = down.total()[0]
     up_share = up.total()[0]
-    out_share, qkv_share, table_share, *norm_shares = joined(near, far, width, (buckets // ways, heads))
+    out_share, qkv_share, table_share, *norm_shares = joined(last, width, (heads, 1, buckets // ways))
     return (
         kept["out"][None],
         kept["input_grad"][None],
         qkv_share[None],
         out_share[None],
-        table_share[None],
+        table_share.transpose(1, 2, 0),
         norm_shares[0],
         norm_shares[1],
         up_share[None],

time: 316 us -> 315 us (level)
  starting transfers between devices: 23.8 us -> 19.3 us
    ppermute x16 -> x12, starting transfers between devices: 18.6 us -> 14.1 us  [swap(): lax.ppermute(theirs, 'dp', [(i, i ^ 1 << bit) for i in range(count)])]
    ppermute x16 -> x12, waiting for transfers between devices: 54.4 us -> 58.4 us  [swap(): lax.ppermute(theirs, 'dp', [(i, i ^ 1 << bit) for i in range(count)])]
    unnamed x46 -> x48, local copies, waits for them, and re-layouts: 10.6 us -> 9.38 us
  transfers between devices with their start and end apart: 20 -> 16, of which waited for: 11 -> 9; matrix products, arithmetic and copies ran while one was open for 5% -> 5% of each run, Pallas kernels for 30% -> 30%
where the time goes in v2:
time: 315 us; the launch traced here: 313 us
  Pallas kernels  139 us (44%)
  waiting for transfers between devices  116 us (37%)
  matrix products  23.2 us (7%)
  starting transfers between devices  19.3 us (6%)
  local copies, waits for them, and re-layouts  11.9 us (4%)
    pallas_call x8, Pallas kernels, layer_step(): pl.pallas_call(functools.partial(layer_kernel, work, phase_on, block, INS...  129 us
    ppermute x12, waiting for transfers between devices, swap(): lax.ppermute(theirs, 'dp', [(i, i ^ 1 << bit) for i in range(count)])  58.4 us
    ppermute x4, waiting for transfers between devices, passed_along(): return lax.ppermute(x, axis, pairs)  58 us
    dot_general x5, matrix products, dot_tn(): lax.dot_general(a, b, (((0,), (0,)), ((), ())), preferred_element_type=F32)  23.2 us
    ppermute x12, starting transfers between devices, swap(): lax.ppermute(theirs, 'dp', [(i, i ^ 1 << bit) for i in range(count)])  14.1 us
    unnamed x48, local copies, waits for them, and re-layouts  9.38 us
    pallas_call x7, Pallas kernels, halve_all(): pl.pallas_call(functools.partial(halve_kernel, tuple(bits), tuple(counts)...  7.8 us
  transfers between devices with their start and end apart: 16, of which 9 were waited for; matrix products, arithmetic and copies ran while one was open for 5% of the time, Pallas kernels for 30%

profile of v2, /device:TPU:0, one launch (start us, length us, event | category | flops | bytes accessed | tf_op | source)
XLA Modules:
  0.0 312.7 jit_solution(5697679100929766066)
XLA Ops:
  0.6 24.5 %forward_0_0.1 = (bf16[1024,768]{1,0:T(8,128)(2,1)}, bf16[1024,2304]{1,0:T(8,128)(2,1)}, bf16[2,12,512,512]{3,2,1,0:T(8,128)(2,1)}, bf16[1024,768]{1,0:T(8,128)(...) custom-call(s32[1]{0:T(128)} %bitcast.refs_0_, ...), custom_call_target="tpu_custom_call" | custom-call | tf_op jit(solution)/shard_map/forward_0_0/pallas_call | solution.py:560
  25.1 1.3 collective-permute-start.1
  26.5 1.8 bias_1_0.1
  28.3 25.8 %forward_0_1.1 = (bf16[1024,768]{1,0:T(8,128)(2,1)}, bf16[1024,2304]{1,0:T(8,128)(2,1)}, bf16[2,12,512,512]{3,2,1,0:T(8,128)(2,1)}, bf16[1024,768]{1,0:T(8,128)(...) custom-call(s32[1]{0:T(128)} %bitcast.refs_0_, ...), custom_call_target="tpu_custom_call", output_to_operand_aliasing={{0}: (16, {}), {1}: (17, {}), {2}: (18, {}), {3}: (19, {}),... | custom-call | tf_op jit(solution)/shard_map/forward_0_1/pallas_call | solution.py:560
  54.1 1.3 collective-permute-start
  56.4 11.4 %both_1_0.1 = (bf16[1024,768]{1,0:T(8,128)(2,1)}, bf16[1024,2304]{1,0:T(8,128)(2,1)}, bf16[2,12,512,512]{3,2,1,0:T(8,128)(2,1)}, bf16[1024,768]{1,0:T(8,128)(2,1...) custom-call(s32[1]{0:T(128)} %bitcast.refs_0_, ...), custom_call_target="tpu_custom_call", output_to_operand_aliasing={{0}: (16, {}), {1}: (17, {}), {2}: (18, {}), {3}: (19, {}),... | custom-call | tf_op jit(solution)/shard_map/both_1_0/pallas_call | solution.py:560
  69.1 4.3 %collective-permute-done.refs_3_ = bf16[512,768]{1,0:T(8,128)(2,1)S(1)} collective-permute-done((bf16[512,768]{1,0:T(8,128)(2,1)}, bf16[512,768]{1,0:T(8,128)(2,1)S(1)}, u32[]{:S(2)}, u32[]{:S(2)}) %collective-permute-start) | collective-permute-done | bytes 786464 | tf_op jit(solution)/shard_map/ppermute | solution.py:785
  74.3 1.9 both_1_1.1
  77.5 41.4 %collective-permute-done.3.refs_3_ = bf16[512,768]{1,0:T(8,128)(2,1)S(1)} collective-permute-done((bf16[512,768]{1,0:T(8,128)(2,1)}, bf16[512,768]{1,0:T(8,128)(2,1)S(1)}, u32[]{:S(2)}, u32[]{:S(2)}) %collective-permute-start.3) | collective-permute-done | bytes 786464 | tf_op jit(solution)/shard_map/ppermute | solution.py:785
  119.8 31.9 %back_0_0.1 = (bf16[1024,768]{1,0:T(8,128)(2,1)}, bf16[1024,2304]{1,0:T(8,128)(2,1)}, bf16[2,12,512,512]{3,2,1,0:T(8,128)(2,1)}, bf16[1024,768]{1,0:T(8,128)(2,1...) custom-call(s32[1]{0:T(128)} %bitcast.refs_0_, ...), custom_call_target="tpu_custom_call", output_to_operand_aliasing={{0}: (16, {}), {1}: (17, {}), {2}: (18, {}), {3}: (19, {}),... | custom-call | tf_op jit(solution)/shard_map/back_0_0/pallas_call | solution.py:560
  151.8 12.3 %collective-permute-done.2.refs_3_ = bf16[512,768]{1,0:T(8,128)(2,1)S(1)} collective-permute-done((bf16[512,768]{1,0:T(8,128)(2,1)}, bf16[512,768]{1,0:T(8,128)(2,1)S(1)}, u32[]{:S(2)}, u32[]{:S(2)}) %collective-permute-start.2) | collective-permute-done | bytes 786464 | tf_op jit(solution)/shard_map/ppermute | solution.py:785
  165.0 15.1 %ffn_back_0_1.1 = (bf16[1024,768]{1,0:T(8,128)(2,1)}, bf16[1024,2304]{1,0:T(8,128)(2,1)}, bf16[2,12,512,512]{3,2,1,0:T(8,128)(2,1)}, bf16[1024,768]{1,0:T(8,128)...) custom-call(s32[1]{0:T(128)} %bitcast.refs_0_, ...), custom_call_target="tpu_custom_call", output_to_operand_aliasing={{0}: (16, {}), {1}: (17, {}), {2}: (18, {}), {3}: (19, {}),... | custom-call | tf_op jit(solution)/shard_map/ffn_back_0_1/pallas_call | solution.py:560
  180.0 7.8 %convolution_convert_fusion = bf16[768,3072]{1,0:T(8,128)(2,1)S(1)} fusion(bf16[1024,768]{1,0:T(8,128)(2,1)} %get-tuple-element.341.refs_24_, bf16[1024,3072]{1,0:T(8,128)(2,1)} %get-tuple-element.342.refs_32_), kind=kOutput, calls=%fused_computation | convolution fusion | flops 4834197504 | bytes 12582912 | tf_op jit(solution)/shard_map/dot_general | solution.py:45
  189.3 5.5 %convolution_convert_fusion.1 = bf16[3072,768]{1,0:T(8,128)(2,1)S(1)} fusion(bf16[1024,3072]{1,0:T(8,128)(2,1)S(1)} %copy-done.14, bf16[1024,768]{1,0:T(8,128)(2,1)S(1)} %copy-done.16), kind=kOutput, calls=%fused_computation.1 | convolution fusion | flops 4834197504 | bytes 12582912 | tf_op jit(solution)/shard_map/dot_general | solution.py:45
  196.1 1.4 copy-done.5
  197.5 1.8 collective-permute-start.7
  200.4 1.8 collective-permute-start.6
  202.2 1.5 convolution_convert_fusion.3
  204.6 16.1 %attn_back_0_1.1 = (bf16[1024,768]{1,0:T(8,128)(2,1)}, bf16[1024,2304]{1,0:T(8,128)(2,1)}, bf16[2,12,512,512]{3,2,1,0:T(8,128)(2,1)}, bf16[1024,768]{1,0:T(8,128...) custom-call(s32[1]{0:T(128)} %bitcast.refs_0_, ...), custom_call_target="tpu_custom_call", output_to_operand_aliasing={{0}: (18, {}), {1}: (19, {}), {2}: (20, {}), {3}: (21, {}),... | custom-call | tf_op jit(solution)/shard_map/attn_back_0_1/pallas_call | solution.py:560
  223.4 1.5 pack.1
  224.9 5.0 %convolution_convert_fusion.2 = bf16[768,1536]{1,0:T(8,128)(2,1)S(1)} fusion(bf16[1024,768]{1,0:T(8,128)(2,1)} %get-tuple-element.366.refs_5_, bf16[1024,2304]{1,0:T(8,128)(2,1)} %get-tuple-element.367), kind=kOutput, calls=%fused_computation.2 | convolution fusion | flops 2417098752 | bytes 7077888 | tf_op jit(solution)/shard_map/dot_general | solution.py:45
  231.7 4.4 %halve.9 = (bf16[2,1,192,768]{3,2,1,0:T(8,128)(2,1)}, f32[2,1,192,768]{3,2,1,0:T(8,128)}, bf16[1,2,48,3072]{3,2,1,0:T(8,128)(2,1)}, f32[1,2,48,3072]{3,2,1,0:T(8,128)}, bf16[1024,768]{1,0:T(8,128)(2,1)}) custom-call(s32[1]{0:T(128)} %bitcast.4.me_ref, f32[2,2,1,192,768]{4,3,2,1,0:T(8,128)} %bitcast.89, ...), custom_call_target="tpu_custom_call", output_to_operand_aliasing={{4}: (6, {})} | custom-call | tf_op jit(solution)/shard_map/halve/pallas_call | solution.py:747
  236.1 3.4 %fusion.3 = bf16[768,768]{1,0:T(8,128)(2,1)S(1)} fusion(bf16[1024,768]{1,0:T(8,128)(2,1)} %get-tuple-element.368, bf16[1024,2304]{1,0:T(8,128)(2,1)} %get-tuple-element.367), kind=kOutput, calls=%fused_computation.9 | convolution fusion | flops 1208549376 | bytes 4325376 | tf_op jit(solution)/shard_map/dot_general | solution.py:45
  239.9 4.7 %collective-permute-done.8 = bf16[8,48,3200]{2,1,0:T(8,128)(2,1)S(1)} collective-permute-done((bf16[8,48,3200]{2,1,0:T(8,128)(2,1)S(1)}, bf16[8,48,3200]{2,1,0:T(8,128)(2,1)S(1)}, u32[]{:S(2)}, u32[]{:S(2)}) %collective-permute-start.8) | collective-permute-done | bytes 2457632 | tf_op jit(solution)/shard_map/ppermute | solution.py:688
  245.6 1.4 collective-permute-start.9
  247.0 1.6 collective-permute-start.10
  248.6 2.6 collective-permute-start.11
  251.1 23.5 %collective-permute-done.10 = bf16[2,192,768]{2,1,0:T(8,128)(2,1)S(1)} collective-permute-done((bf16[2,192,768]{2,1,0:T(8,128)(2,1)S(1)}, bf16[2,192,768]{2,1,0:T(8,128)(2,1)S(1)}, u32[]{:S(2)}, u32[]{:S(2)}) %collective-permute-start.10) | collective-permute-done | bytes 589856 | tf_op jit(solution)/shard_map/ppermute | solution.py:688
  274.6 2.3 collective-permute-done.11
  278.7 2.6 collective-permute-start.15
  281.3 16.0 %collective-permute-done.12 = bf16[2,48,3200]{2,1,0:T(8,128)(2,1)S(1)} collective-permute-done((bf16[2,48,3200]{2,1,0:T(8,128)(2,1)S(1)}, bf16[2,48,3200]{2,1,0:T(8,128)(2,1)S(1)}, u32[]{:S(2)}, u32[]{:S(2)}) %collective-permute-start.12) | collective-permute-done | bytes 614432 | tf_op jit(solution)/shard_map/ppermute | solution.py:688
  300.0 11.6 %collective-permute-done.13 = bf16[1,48,3200]{2,1,0:T(8,128)(2,1)S(1)} collective-permute-done((bf16[1,48,3200]{2,1,0:T(8,128)(2,1)S(1)}, bf16[1,48,3200]{2,1,0:T(8,128)(2,1)S(1)}, u32[]{:S(2)}, u32[]{:S(2)}) %collective-permute-start.13) | collective-permute-done | bytes 307232 | tf_op jit(solution)/shard_map/ppermute | solution.py:688
  (79 shorter events, 21.8 us)
Async XLA Ops:
  25.1 30.3 %collective-permute-start.1 = (bf16[512,768]{1,0:T(8,128)(2,1)}, bf16[512,768]{1,0:T(8,128)(2,1)S(1)}, u32[]{:S(2)}, u32[]{:S(2)}) collective-permute-start(bf16[512,768]{1,0:T(8,128)(2,1)} %get-tuple-element.247), channel_id=1, source_target_pairs={{0,16},{1,17},{2,18},{3,19},{4,20},{5,21},{6,22},{7,23},{8,24},{9,... | collective-permute-start | bytes 2359304 | tf_op jit(solution)/shard_map/ppermute | solution.py:785
  54.1 19.3 %collective-permute-start = (bf16[512,768]{1,0:T(8,128)(2,1)}, bf16[512,768]{1,0:T(8,128)(2,1)S(1)}, u32[]{:S(2)}, u32[]{:S(2)}) collective-permute-start(bf16[512,768]{1,0:T(8,128)(2,1)} %get-tuple-element.246), channel_id=1, source_target_pairs={{0,16},{1,17},{2,18},{3,19},{4,20},{5,21},{6,22},{7,23},{8,24},{9,... | collective-permute-start | bytes 2359304 | tf_op jit(solution)/shard_map/ppermute | solution.py:785
  67.8 51.2 %collective-permute-start.3 = (bf16[512,768]{1,0:T(8,128)(2,1)}, bf16[512,768]{1,0:T(8,128)(2,1)S(1)}, u32[]{:S(2)}, u32[]{:S(2)}) collective-permute-start(bf16[512,768]{1,0:T(8,128)(2,1)} %get-tuple-element.293), channel_id=1, source_target_pairs={{16,0},{17,1},{18,2},{19,3},{20,4},{21,5},{22,6},{23,7},{24,8},{25... | collective-permute-start | bytes 2359304 | tf_op jit(solution)/shard_map/ppermute | solution.py:785
  76.2 87.9 %collective-permute-start.2 = (bf16[512,768]{1,0:T(8,128)(2,1)}, bf16[512,768]{1,0:T(8,128)(2,1)S(1)}, u32[]{:S(2)}, u32[]{:S(2)}) collective-permute-start(bf16[512,768]{1,0:T(8,128)(2,1)} %get-tuple-element.292), channel_id=1, source_target_pairs={{16,0},{17,1},{18,2},{19,3},{20,4},{21,5},{22,6},{23,7},{24,8},{25... | collective-permute-start | bytes 2359304 | tf_op jit(solution)/shard_map/ppermute | solution.py:785
  180.0 8.1 %copy-start.14 = (bf16[1024,3072]{1,0:T(8,128)(2,1)S(1)}, bf16[1024,3072]{1,0:T(8,128)(2,1)}, u32[]{:S(2)}) copy-start(bf16[1024,3072]{1,0:T(8,128)(2,1)} %get-tuple-element.338.refs_26_) | copy-start | bytes 18874372
  187.9 1.4 copy-start.16
  188.1 7.0 %collective-permute-start.5 = (bf16[8,48,3072]{2,1,0:T(8,128)(2,1)S(1)}, bf16[8,48,3072]{2,1,0:T(8,128)(2,1)S(1)}, u32[]{:S(2)}, u32[]{:S(2)}) collective-permute-start(bf16[8,48,3072]{2,1,0:T(8,128)(2,1)S(1)} %dynamic-slice_bitcast_fusion), channel_id=1, source_target_pairs={{0,1},{1,0},{2,3},{3,2},{4,5},{5,4},{6,7},{7,6},{8,9},{9,8},{10,11... | collective-permute-start | bytes 7077896 | tf_op jit(solution)/shard_map/ppermute | solution.py:688
  195.0 4.6 %collective-permute-start.4 = (bf16[8,192,768]{2,1,0:T(8,128)(2,1)S(1)}, bf16[8,192,768]{2,1,0:T(8,128)(2,1)S(1)}, u32[]{:S(2)}, u32[]{:S(2)}) collective-permute-start(bf16[8,192,768]{2,1,0:T(8,128)(2,1)S(1)} %dynamic-slice_bitcast_fusion.1), channel_id=1, source_target_pairs={{0,1},{1,0},{2,3},{3,2},{4,5},{5,4},{6,7},{7,6},{8,9},{9,8},{10,11... | collective-permute-start | bytes 7077896 | tf_op jit(solution)/shard_map/ppermute | solution.py:688
  197.5 2.9 copy-start.9
  197.5 33.7 %collective-permute-start.7 = (bf16[4,48,3072]{2,1,0:T(8,128)(2,1)S(1)}, bf16[4,48,3072]{2,1,0:T(8,128)(2,1)}, u32[]{:S(2)}, u32[]{:S(2)}) collective-permute-start(bf16[4,48,3072]{2,1,0:T(8,128)(2,1)S(1)} %bitcast.96), channel_id=1, source_target_pairs={{0,4},{1,5},{2,6},{3,7},{4,0},{5,1},{6,2},{7,3},{8,12},{9,13},{10,... | collective-permute-start | bytes 3538952 | tf_op jit(solution)/shard_map/ppermute | solution.py:688
  199.6 2.6 copy-start.15
  199.6 2.6 copy-start.17
  200.4 3.3 %copy-start.6 = (f32[4,1,192,768]{3,2,1,0:T(8,128)}, f32[4,1,192,768]{3,2,1,0:T(8,128)S(1)}, u32[]{:S(2)}) copy-start(f32[4,1,192,768]{3,2,1,0:T(8,128)S(1)} %get-tuple-element.364) | copy-start | bytes 7077892
  200.4 3.3 %copy-start.10 = (bf16[4,1,192,768]{3,2,1,0:T(8,128)(2,1)}, bf16[4,1,192,768]{3,2,1,0:T(8,128)(2,1)S(1)}, u32[]{:S(2)}) copy-start(bf16[4,1,192,768]{3,2,1,0:T(8,128)(2,1)S(1)} %get-tuple-element.340) | copy-start | bytes 3538948
  200.4 30.8 %collective-permute-start.6 = (bf16[4,192,768]{2,1,0:T(8,128)(2,1)S(1)}, bf16[4,192,768]{2,1,0:T(8,128)(2,1)}, u32[]{:S(2)}, u32[]{:S(2)}) collective-permute-start(bf16[4,192,768]{2,1,0:T(8,128)(2,1)S(1)} %bitcast.98), channel_id=1, source_target_pairs={{0,2},{1,3},{2,0},{3,1},{4,6},{5,7},{6,4},{7,5},{8,10},{9,11},{10,... | collective-permute-start | bytes 3538952 | tf_op jit(solution)/shard_map/ppermute | solution.py:688
  204.6 16.1 %copy-start.13 = (s32[1023]{0:T(1024)S(1)}, s32[1023]{0:T(1024)}, u32[]{:S(2)}) copy-start(s32[1023]{0:T(1024)} %param.27) | copy-start | bytes 12280
  230.0 1.7 copy-start.1
  236.1 3.5 %copy-start.18 = (bf16[8,48,1536]{2,1,0:T(8,128)(2,1)S(1)}, bf16[8,48,1536]{2,1,0:T(8,128)(2,1)}, u32[]{:S(2)}) copy-start(bf16[8,48,1536]{2,1,0:T(8,128)(2,1)} %dynamic-slice_bitcast_fusion.2) | copy-start | bytes 3538948
  236.1 3.5 %copy-start.19 = (bf16[8,48,768]{2,1,0:T(8,128)(2,1)S(1)}, bf16[8,48,768]{2,1,0:T(8,128)(2,1)}, u32[]{:S(2)}) copy-start(bf16[8,48,768]{2,1,0:T(8,128)(2,1)} %dynamic-slice_bitcast_fusion.4) | copy-start | bytes 1769476
  239.6 5.0 %copy-start.2 = (bf16[768,1536]{1,0:T(8,128)(2,1)S(1)}, bf16[768,1536]{1,0:T(8,128)(2,1)}, u32[]{:S(2)}) copy-start(bf16[768,1536]{1,0:T(8,128)(2,1)} %copy-done.1) | copy-start | bytes 7077892
  239.6 5.0 %copy-start.11 = (bf16[1,2,48,3072]{3,2,1,0:T(8,128)(2,1)S(1)}, bf16[1,2,48,3072]{3,2,1,0:T(8,128)(2,1)}, u32[]{:S(2)}) copy-start(bf16[1,2,48,3072]{3,2,1,0:T(8,128)(2,1)} %get-tuple-element.373) | copy-start | bytes 1769476
  239.7 4.9 %copy-start.12 = (bf16[2,1,192,768]{3,2,1,0:T(8,128)(2,1)S(1)}, bf16[2,1,192,768]{3,2,1,0:T(8,128)(2,1)}, u32[]{:S(2)}) copy-start(bf16[2,1,192,768]{3,2,1,0:T(8,128)(2,1)} %get-tuple-element.372) | copy-start | bytes 1769476
  239.8 4.7 %collective-permute-start.8 = (bf16[8,48,3200]{2,1,0:T(8,128)(2,1)S(1)}, bf16[8,48,3200]{2,1,0:T(8,128)(2,1)S(1)}, u32[]{:S(2)}, u32[]{:S(2)}) collective-permute-start(bf16[8,48,3200]{2,1,0:T(8,128)(2,1)S(1)} %pad_maximum_fusion), channel_id=1, source_target_pairs={{0,1},{1,0},{2,3},{3,2},{4,5},{5,4},{6,7},{7,6},{8,9},{9,8},{10,11... | collective-permute-start | bytes 7372808 | tf_op jit(solution)/shard_map/ppermute | solution.py:688
  244.6 32.4 %copy-start.7 = (f32[2,1,192,768]{3,2,1,0:T(8,128)S(1)}, f32[2,1,192,768]{3,2,1,0:T(8,128)}, u32[]{:S(2)}) copy-start(f32[2,1,192,768]{3,2,1,0:T(8,128)} %get-tuple-element.376) | copy-start | bytes 3538948
  244.6 32.4 %copy-start.8 = (f32[1,2,48,3072]{3,2,1,0:T(8,128)S(1)}, f32[1,2,48,3072]{3,2,1,0:T(8,128)}, u32[]{:S(2)}) copy-start(f32[1,2,48,3072]{3,2,1,0:T(8,128)} %get-tuple-element.377) | copy-start | bytes 3538948
  245.6 31.6 %collective-permute-start.9 = (bf16[4,48,3200]{2,1,0:T(8,128)(2,1)S(1)}, bf16[4,48,3200]{2,1,0:T(8,128)(2,1)S(1)}, u32[]{:S(2)}, u32[]{:S(2)}) collective-permute-start(bf16[4,48,3200]{2,1,0:T(8,128)(2,1)S(1)} %bitcast.122), channel_id=1, source_target_pairs={{0,2},{1,3},{2,0},{3,1},{4,6},{5,7},{6,4},{7,5},{8,10},{9,11},{10,... | collective-permute-start | bytes 3686408 | tf_op jit(solution)/shard_map/ppermute | solution.py:688
  247.0 27.6 %collective-permute-start.10 = (bf16[2,192,768]{2,1,0:T(8,128)(2,1)S(1)}, bf16[2,192,768]{2,1,0:T(8,128)(2,1)S(1)}, u32[]{:S(2)}, u32[]{:S(2)}) collective-permute-start(bf16[2,192,768]{2,1,0:T(8,128)(2,1)S(1)} %bitcast.105), channel_id=1, source_target_pairs={{0,4},{1,5},{2,6},{3,7},{4,0},{5,1},{6,2},{7,3},{8,12},{9,13},{10,... | collective-permute-start | bytes 1769480 | tf_op jit(solution)/shard_map/ppermute | solution.py:688
  248.6 28.4 %collective-permute-start.11 = (bf16[2,48,3072]{2,1,0:T(8,128)(2,1)S(1)}, bf16[2,48,3072]{2,1,0:T(8,128)(2,1)S(1)}, u32[]{:S(2)}, u32[]{:S(2)}) collective-permute-start(bf16[2,48,3072]{2,1,0:T(8,128)(2,1)S(1)} %bitcast.103), channel_id=1, source_target_pairs={{0,8},{1,9},{2,10},{3,11},{4,12},{5,13},{6,14},{7,15},{8,0},{9,1},... | collective-permute-start | bytes 1769480 | tf_op jit(solution)/shard_map/ppermute | solution.py:688
  277.5 19.8 %collective-permute-start.12 = (bf16[2,48,3200]{2,1,0:T(8,128)(2,1)S(1)}, bf16[2,48,3200]{2,1,0:T(8,128)(2,1)S(1)}, u32[]{:S(2)}, u32[]{:S(2)}) collective-permute-start(bf16[2,48,3200]{2,1,0:T(8,128)(2,1)S(1)} %bitcast.123), channel_id=1, source_target_pairs={{0,4},{1,5},{2,6},{3,7},{4,0},{5,1},{6,2},{7,3},{8,12},{9,13},{10,... | collective-permute-start | bytes 1843208 | tf_op jit(solution)/shard_map/ppermute | solution.py:688
  278.0 20.3 %collective-permute-start.14 = (bf16[1,48,3072]{2,1,0:T(8,128)(2,1)S(1)}, bf16[1,48,3072]{2,1,0:T(8,128)(2,1)S(1)}, u32[]{:S(2)}, u32[]{:S(2)}) collective-permute-start(bf16[1,48,3072]{2,1,0:T(8,128)(2,1)S(1)} %bitcast.121), channel_id=1, source_target_pairs={{0,2},{1,3},{2,0},{3,1},{4,6},{5,7},{6,4},{7,5},{8,10},{9,11},{10,... | collective-permute-start | bytes 884744 | tf_op jit(solution)/shard_map/ppermute | solution.py:688
  278.7 20.5 %collective-permute-start.15 = (bf16[1,192,768]{2,1,0:T(8,128)(2,1)S(1)}, bf16[1,192,768]{2,1,0:T(8,128)(2,1)S(1)}, u32[]{:S(2)}, u32[]{:S(2)}) collective-permute-start(bf16[1,192,768]{2,1,0:T(8,128)(2,1)S(1)} %bitcast.119), channel_id=1, source_target_pairs={{0,8},{1,9},{2,10},{3,11},{4,12},{5,13},{6,14},{7,15},{8,0},{9,1},... | collective-permute-start | bytes 884744 | tf_op jit(solution)/shard_map/ppermute | solution.py:688
  297.4 14.2 %collective-permute-start.13 = (bf16[1,48,3200]{2,1,0:T(8,128)(2,1)S(1)}, bf16[1,48,3200]{2,1,0:T(8,128)(2,1)S(1)}, u32[]{:S(2)}, u32[]{:S(2)}) collective-permute-start(bf16[1,48,3200]{2,1,0:T(8,128)(2,1)S(1)} %bitcast.124), channel_id=1, source_target_pairs={{0,8},{1,9},{2,10},{3,11},{4,12},{5,13},{6,14},{7,15},{8,0},{9,1},... | collective-permute-start | bytes 921608 | tf_op jit(solution)/shard_map/ppermute | solution.py:688
  (8 other events, 7.7 us)
